TPU v7x, 512 devices: a whole 4x8x8 slice. The times are simulated.
512 devices in a mesh: kvh: 8 (over x, core), seq: 64 (over z, y).
Axes of the slice: x: 4, y: 8, z: 8, core: 2. Of those that a mesh axis runs over, the one named last changes fastest.
Arguments:
- queries: bfloat16 [4, 4, 16384], P(None, None, ('kvh', 'seq')), may hold values from -60 to 60
- drafted_key_value: bfloat16 [4, 4, 2, 8, 128], P(None, None, None, 'kvh'), may hold values from -6 to 6
- paged_key_value: bfloat16 [2, 8, 512, 128, 128], P(None, 'kvh', 'seq'), may hold values from -6 to 6
- block_table: int32 [4, 128], replicated, may hold values from -1 to 511, as said below
- page_count: int32 [4], replicated, may hold values from 1 to 128
- tail_fill: int32 [4], replicated, may hold values from 1 to 128
- out_weight: bfloat16 [16384, 16384], P('kvh', 'seq'), may hold values from -0.375 to 0.375
- stream_in: float32 [4, 4, 16384], P(None, None, 'seq'), may hold values from -4 to 4
- norm_gain: float32 [16384], P('seq'), may hold values from 0.1 to 1.9
- gate_up: bfloat16 [2, 26624, 16384], P(None, ('kvh', 'seq')), may hold values from -0.046875 to 0.046875
Outputs:
- hidden: bfloat16 [4, 4, 26624], P(None, None, ('kvh', 'seq'))
- stream: float32 [4, 4, 16384], P(None, None, 'seq')
Inputs may be any that keep to these rules, and one draw needn't show every extreme that they name: `block_table`: each slot stands at most once in the table; entries at pages from page_count on are -1, the others are slots.
All inputs are finite; a program needn't handle non-finite values.
Results may differ from a plain program's by a relative error of at most 0.0095.
Values may be sent and summed in bfloat16 or wider, within the bound.
No kernel may reach another device: no remote copies, remote signals or barrier semaphores. Data moves between devices by JAX's collectives and lax.ppermute only.
A program may use at most 64 MiB of HBM per device.

v0:
```python
import jax
import jax.numpy as jnp
from jax import lax
from jax.sharding import PartitionSpec as P

QUERY_HEADS = 128
KEY_VALUE_HEADS = 8


big_negative = -1e30
epsilon = 1e-05


def slot_layout(block_table, page_count, tail_fill, seq_index, pages_dev, page_len):
    most = block_table.shape[1]
    slot_ids = seq_index * pages_dev + jnp.arange(pages_dev, dtype=jnp.int32)
    page_index = jnp.arange(most, dtype=jnp.int32)
    held = (block_table[:, :, None] == slot_ids[None, None, :]) & (
        page_index[None, :, None] < page_count[:, None, None]
    )
    owner = jnp.any(held, axis=1)
    owner_int = owner.astype(jnp.int32)
    which_page = jnp.sum(held.astype(jnp.int32) * page_index[None, :, None], axis=(0, 1))
    count_of = jnp.sum(owner_int * page_count[:, None], axis=0)
    tail_of = jnp.sum(owner_int * tail_fill[:, None], axis=0)
    live = jnp.any(owner, axis=0)
    filled = jnp.where(which_page < count_of - 1, page_len, tail_of)
    return (owner, jnp.where(live, filled, 0))


def local_partials(queries, cache, fresh, owner, filled, seq_index, seq_count):
    steps, rows, heads, query_group, width = queries.shape
    page_len = cache.shape[3]
    scale = width ** (-0.5)
    slot_q = jnp.einsum(
        "rp,srhgd->pshgd", owner.astype(jnp.bfloat16), queries, preferred_element_type=jnp.float32
    ).astype(jnp.bfloat16)
    cache_scores = (
        jnp.einsum("pshgd,hpld->pshgl", slot_q, cache[0], preferred_element_type=jnp.float32)
        * scale
    )
    valid = jnp.arange(page_len)[None, :] < filled[:, None]
    valid_wide = valid[:, None, None, None, :]
    cache_scores = jnp.where(valid_wide, cache_scores, big_negative)
    slot_max = jnp.max(cache_scores, axis=4)
    row_cache_max = jnp.max(
        jnp.where(owner[:, :, None, None, None], slot_max[None], big_negative), axis=1
    )
    mine = jnp.arange(rows) % seq_count == seq_index
    fresh_scores = (
        jnp.einsum("srhgd,urhd->rshgu", queries, fresh[:, :, 0], preferred_element_type=jnp.float32)
        * scale
    )
    causal = jnp.arange(steps)[None, :] <= jnp.arange(steps)[:, None]
    fresh_ok = mine[:, None, None, None, None] & causal[None, :, None, None, :]
    fresh_scores = jnp.where(fresh_ok, fresh_scores, big_negative)
    row_max = jnp.maximum(row_cache_max, jnp.max(fresh_scores, axis=4))
    owner_index = jnp.sum(
        owner.astype(jnp.int32) * jnp.arange(rows, dtype=jnp.int32)[:, None], axis=0
    )
    slot_peak = row_max[owner_index]
    cache_weights = jnp.where(valid_wide, jnp.exp(cache_scores - slot_peak[..., None]), 0.0)
    fresh_weights = jnp.where(fresh_ok, jnp.exp(fresh_scores - row_max[..., None]), 0.0)
    owner_float = owner.astype(jnp.float32)
    total = jnp.einsum(
        "rp,pshg->rshg",
        owner_float,
        jnp.sum(cache_weights, axis=4),
        precision=lax.Precision.HIGHEST,
    )
    total = total + jnp.sum(fresh_weights, axis=4)
    slot_out = jnp.einsum(
        "pshgl,hpld->pshgd",
        cache_weights,
        cache[1].astype(jnp.float32),
        precision=lax.Precision.HIGHEST,
    )
    numer = jnp.einsum("rp,pshgd->rshgd", owner_float, slot_out, precision=lax.Precision.HIGHEST)
    numer = numer + jnp.einsum(
        "rshgu,urhd->rshgd",
        fresh_weights,
        fresh[:, :, 1].astype(jnp.float32),
        precision=lax.Precision.HIGHEST,
    )
    count = steps * rows
    row_max = jnp.transpose(row_max, (1, 0, 2, 3)).reshape(count, heads * query_group)
    total = jnp.transpose(total, (1, 0, 2, 3)).reshape(count, heads * query_group)
    numer = jnp.transpose(numer, (1, 0, 2, 3, 4)).reshape(count, heads * query_group, width)
    return (row_max, total, numer)


def shards(
    queries,
    drafted_key_value,
    paged_key_value,
    block_table,
    page_count,
    tail_fill,
    out_weight,
    stream_in,
    norm_gain,
    gate_up,
):
    steps, rows = (queries.shape[0], queries.shape[1])
    count = steps * rows
    seq_count = lax.axis_size("seq")
    seq_index = lax.axis_index("seq")
    heads_here = paged_key_value.shape[1]
    query_group = QUERY_HEADS // KEY_VALUE_HEADS
    width = paged_key_value.shape[4]
    features = heads_here * query_group * width
    whole_queries = lax.all_gather(queries, "seq", axis=2, tiled=True).reshape(
        steps, rows, heads_here, query_group, width
    )
    owner, filled = slot_layout(
        block_table,
        page_count,
        tail_fill,
        seq_index,
        paged_key_value.shape[2],
        paged_key_value.shape[3],
    )
    row_max, total, numer = local_partials(
        whole_queries, paged_key_value, drafted_key_value, owner, filled, seq_index, seq_count
    )
    columns_here = out_weight.shape[1]
    slice_width = features // seq_count
    per_slice = 1
    repeat = width // slice_width

    def by_slice(stat):
        spread = jnp.repeat(stat, repeat, axis=1)
        return jnp.transpose(spread.reshape(count, seq_count, per_slice), (1, 0, 2))

    pieces = jnp.transpose(numer.reshape(count, seq_count, slice_width), (1, 0, 2))
    got_values, got_max, got_total = (
        lax.all_to_all(pieces, "seq", split_axis=0, concat_axis=0, tiled=True),
        lax.all_to_all(by_slice(row_max), "seq", split_axis=0, concat_axis=0, tiled=True),
        lax.all_to_all(by_slice(total), "seq", split_axis=0, concat_axis=0, tiled=True),
    )
    peak = jnp.max(got_max, axis=0)
    factor = jnp.exp(got_max - peak[None])
    summed_total = jnp.sum(factor * got_total, axis=0)
    shaped = got_values.reshape(seq_count, count, per_slice, slice_width // per_slice)
    combined = jnp.sum(shaped * factor[..., None], axis=0)
    attended = (combined / summed_total[..., None]).reshape(count, slice_width).astype(jnp.bfloat16)
    block = out_weight
    partial_sum = jnp.dot(
        lax.all_gather(attended, "seq", axis=1, tiled=True),
        block,
        preferred_element_type=jnp.float32,
    )
    projected = lax.psum(partial_sum, "kvh")
    stream = stream_in.reshape(count, columns_here) + projected
    model_width = columns_here * seq_count
    units_here = gate_up.shape[1]
    squares = lax.psum(jnp.sum(stream * stream, axis=1), "seq")
    scaled = (stream * norm_gain[None, :]).astype(jnp.bfloat16)
    block = gate_up
    both = jnp.einsum(
        "nc,kfc->knf",
        lax.all_gather(scaled, "seq", axis=1, tiled=True),
        block,
        preferred_element_type=jnp.float32,
    )
    inverse = lax.rsqrt(squares / model_width + epsilon)
    both = both * inverse[None, :, None]
    hidden = (jax.nn.silu(both[0]) * both[1]).astype(jnp.bfloat16)
    return (hidden.reshape(steps, rows, units_here), stream.reshape(steps, rows, columns_here))


def solution(mesh):
    placed = (
        P(None, None, ("kvh", "seq")),
        P(None, None, None, "kvh", None),
        P(None, "kvh", "seq", None, None),
        P(),
        P(),
        P(),
        P("kvh", "seq"),
        P(None, None, "seq"),
        P("seq"),
        P(None, ("kvh", "seq"), None),
    )
    return jax.shard_map(
        shards,
        mesh=mesh,
        in_specs=placed,
        out_specs=(P(None, None, ("kvh", "seq")), P(None, None, "seq")),
        check_vma=False,
    )
```

profile of v0, /device:TPU:56, one launch (start us, length us, event | category | flops | bytes accessed | tf_op | source)
XLA Modules:
  0.0 407.7 jit_solution(7595928967461347211)
XLA Ops:
  0.7 0.9 iota_compare_fusion.2
  1.6 1.0 select_reduce_fusion.1
  2.6 1.0 fusion.40
  4.4 61.5 %all_gather.9 = bf16[4,4,2048]{1,0,2:T(4,128)(2,1)} all-gather(bf16[4,4,32]{1,0,2:T(4,128)(2,1)S(1)} %copy.99), channel_id=1, replica_groups=mesh['kvh'=8,'seq'=64] {'seq'}, dimensions={2}, use_global_device_ids=true | all-gather | bytes 66560 | tf_op jit(solution)/shard_map/all_gather | solution.py:112
  66.0 2.6 copy.105
  68.6 2.3 fusion.5
  71.7 1.9 fusion.55
  75.4 1.2 fusion.28
  77.5 8.8 %all-to-all-start.2 = ((f32[64,16,1]{1,2,0:T(1,128)}), f32[64,16,1]{1,2,0:T(1,128)}, u32[]{:S(2)}, u32[]{:S(2)}) async-start(f32[64,16,1]{1,2,0:T(1,128)} %bitcast.44), calls=%async_computation.2 | async-start | bytes 65536 | tf_op jit(solution)/shard_map/all_to_all | solution.py:139
  86.3 2.1 fusion.21
  88.4 1.2 fusion.33
  89.7 6.1 %all-to-all-done.2 = f32[64,16,1]{1,2,0:T(1,128)} async-done(((f32[64,16,1]{1,2,0:T(1,128)}), f32[64,16,1]{1,2,0:T(1,128)}, u32[]{:S(2)}, u32[]{:S(2)}) %all-to-all-start.2) | async-done | bytes 4128 | tf_op jit(solution)/shard_map/all_to_all | solution.py:139
  96.4 7.5 %all-to-all-start.1 = ((f32[64,16,1]{1,2,0:T(1,128)}), f32[64,16,1]{1,2,0:T(1,128)}, u32[]{:S(2)}, u32[]{:S(2)}) async-start(f32[64,16,1]{1,2,0:T(1,128)} %bitcast.129), calls=%async_computation.1 | async-start | bytes 65536 | tf_op jit(solution)/shard_map/all_to_all | solution.py:138
  103.9 1.4 fusion.11
  105.3 1.0 reshape_reshape.9
  106.3 2.1 copy.110
  108.4 1.9 reshape.276
  110.4 3.1 all-to-all-done.1
  113.5 9.7 %all-to-all-start = ((f32[64,1,512]{2,1,0:T(1,128)}), f32[64,1,512]{2,1,0:T(1,128)S(1)}, u32[]{:S(2)}, u32[]{:S(2)}) async-start(f32[64,1,512]{2,1,0:T(1,128)} %reshape.276), calls=%async_computation | async-start | bytes 262144 | tf_op jit(solution)/shard_map/all_to_all | solution.py:137
  123.9 1.4 reduce_max.39
  125.2 1.9 multiply_reduce_fusion.1
  127.2 5.8 %all-to-all-done = f32[64,1,512]{2,1,0:T(1,128)S(1)} async-done(((f32[64,1,512]{2,1,0:T(1,128)}), f32[64,1,512]{2,1,0:T(1,128)S(1)}, u32[]{:S(2)}, u32[]{:S(2)}) %all-to-all-start) | async-done | bytes 131104 | tf_op jit(solution)/shard_map/all_to_all | solution.py:137
  134.2 1.9 reduce.10
  136.0 1.0 reshape.277
  137.0 1.2 multiply_reduce_fusion
  139.0 49.3 %all-gather = bf16[64,32,16]{1,2,0:T(8,128)(2,1)S(1)} all-gather(bf16[1,32,16]{1,2,0:T(8,128)(2,1)S(1)} %fusion.44), channel_id=1, replica_groups=mesh['kvh'=8,'seq'=64] {'seq'}, dimensions={0}, use_global_device_ids=true | all-gather | bytes 66560 | tf_op jit(solution)/shard_map/all_gather | solution.py:149
  189.0 1.2 reshape.268
  190.3 1.5 fusion.57
  191.8 23.6 %psum.14 = f32[16,256]{1,0:T(8,128)S(1)} all-reduce(f32[16,256]{1,0:T(8,128)S(1)} %fusion.57), channel_id=1, replica_groups=mesh['kvh'=8,'seq'=64] {'kvh'}, use_global_device_ids=true, to_apply=%region_14.15 | all-reduce | flops 4096 | bytes 32768 | tf_op jit(solution)/shard_map/psum | solution.py:153
  215.4 128.7 %psum.15 = f32[16]{0:T(128)S(1)} all-reduce(f32[16]{0:T(128)S(1)} %get-tuple-element.7), channel_id=1, replica_groups=mesh['kvh'=8,'seq'=64] {'seq'}, use_global_device_ids=true, to_apply=%region_16.17 | all-reduce | flops 16 | bytes 128 | tf_op jit(solution)/shard_map/psum | solution.py:157
  345.5 59.6 %all_gather.11 = bf16[16,16384]{1,0:T(8,128)(2,1)S(1)} all-gather(bf16[16,256]{1,0:T(8,128)(2,1)S(1)} %multiply_convert_fusion), channel_id=1, replica_groups=mesh['kvh'=8,'seq'=64] {'seq'}, dimensions={1}, use_global_device_ids=true | all-gather | bytes 532480 | tf_op jit(solution)/shard_map/all_gather | solution.py:162
  405.1 2.0 fusion.16
  (48 shorter events, 10.3 us)
Async XLA Ops:
  0.6 404.4 %copy-start = (bf16[2,52,16384]{2,0,1:T(2,128)(2,1)S(1)}, bf16[2,52,16384]{2,0,1:T(2,128)(2,1)}, u32[]{:S(2)}) copy-start(bf16[2,52,16384]{2,0,1:T(2,128)(2,1)} %param.19) | copy-start | bytes 10223620
  0.6 70.3 %copy-start.5 = (s32[4]{0:T(128)S(1)}, s32[4]{0:T(128)}, u32[]{:S(2)}) copy-start(s32[4]{0:T(128)} %param.14) | copy-start | bytes 52
  0.7 70.2 %copy-start.6 = (s32[4]{0:T(128)S(1)}, s32[4]{0:T(128)}, u32[]{:S(2)}) copy-start(s32[4]{0:T(128)} %param.15) | copy-start | bytes 52
  0.7 70.4 %copy-start.3 = (bf16[4,4,2,1,128]{4,2,3,1,0:T(2,128)(2,1)S(1)}, bf16[4,4,2,1,128]{4,2,3,1,0:T(2,128)(2,1)}, u32[]{:S(2)}) copy-start(bf16[4,4,2,1,128]{4,2,3,1,0:T(2,128)(2,1)} %param.11) | copy-start | bytes 24580
  3.6 73.1 %copy-start.4 = (pred[4,8]{1,0:T(4,128)(4,1)}, pred[4,8]{1,0:T(4,128)(4,1)S(1)}, u32[]{:S(2)}) copy-start(pred[4,8]{1,0:T(4,128)(4,1)S(1)} %get-tuple-element.3) | copy-start | bytes 100
  74.1 0.6 copy-start.2
  77.5 18.3 %all-to-all-start.2 = ((f32[64,16,1]{1,2,0:T(1,128)}), f32[64,16,1]{1,2,0:T(1,128)}, u32[]{:S(2)}, u32[]{:S(2)}) async-start(f32[64,16,1]{1,2,0:T(1,128)} %bitcast.44), calls=%async_computation.2 | async-start | bytes 65536 | tf_op jit(solution)/shard_map/all_to_all | solution.py:139
  96.4 17.0 %all-to-all-start.1 = ((f32[64,16,1]{1,2,0:T(1,128)}), f32[64,16,1]{1,2,0:T(1,128)}, u32[]{:S(2)}, u32[]{:S(2)}) async-start(f32[64,16,1]{1,2,0:T(1,128)} %bitcast.129), calls=%async_computation.1 | async-start | bytes 65536 | tf_op jit(solution)/shard_map/all_to_all | solution.py:138
  113.5 19.6 %all-to-all-start = ((f32[64,1,512]{2,1,0:T(1,128)}), f32[64,1,512]{2,1,0:T(1,128)S(1)}, u32[]{:S(2)}, u32[]{:S(2)}) async-start(f32[64,1,512]{2,1,0:T(1,128)} %reshape.276), calls=%async_computation | async-start | bytes 262144 | tf_op jit(solution)/shard_map/all_to_all | solution.py:137
  133.0 0.6 copy-start.1
where the time goes:
time: 409 us; the launch traced here: 408 us
  blocking collectives  323 us (79%)
  starting transfers between devices  26 us (6%)
  local copies, waits for them, and re-layouts  17.2 us (4%)
  waiting for transfers between devices  15.1 us (4%)
  other arithmetic  13.2 us (3%)
  matrix products  12.8 us (3%)
    psum x1, blocking collectives, shards(): squares = lax.psum(jnp.sum(stream * stream, axis=1), 'seq')  129 us
    all_gather x1, blocking collectives, shards(): lax.all_gather(queries, 'seq', axis=2, tiled=True)  61.5 us
    all_gather x1, blocking collectives, shards(): lax.all_gather(scaled, 'seq', axis=1, tiled=True)  59.6 us
    all_gather x1, blocking collectives, shards(): lax.all_gather(attended, 'seq', axis=1, tiled=True)  49.3 us
    psum x1, blocking collectives, shards(): projected = lax.psum(partial_sum, 'kvh')  23.6 us
    all_to_all x1, starting transfers between devices, shards(): lax.all_to_all(pieces, 'seq', split_axis=0, concat_axis=0, tiled=True)  9.68 us
    all_to_all x1, starting transfers between devices, shards(): lax.all_to_all(by_slice(total), 'seq', split_axis=0, concat_axis=0, tiled...  8.81 us
  transfers between devices with their start and end apart: 3, of which 3 were waited for; matrix products, arithmetic and copies ran while one was open for 3% of the time, Pallas kernels for 0%

commit v1 on v0

v1 whole, which is shorter than its diff:
```python
import jax
import jax.numpy as jnp
from jax import lax
from jax.experimental import pallas as pl
from jax.experimental.pallas import tpu as pltpu
from jax.sharding import Mesh
from jax.sharding import PartitionSpec as P

QUERY_HEADS = 128
KEY_VALUE_HEADS = 8
GROUP = QUERY_HEADS // KEY_VALUE_HEADS
WIDTH = 128
STEPS = 4
ROWS = 4
COUNT = STEPS * ROWS
QUARTER = 32
SIDE = 8

low = -1e30
floor = -1e29
epsilon = 1e-05
f32 = jnp.float32
bf16 = jnp.bfloat16


def iota(shape, axis):
    return lax.broadcasted_iota(jnp.int32, shape, axis)


def dot(a, b):
    return lax.dot_general(a, b, (((1,), (0,)), ((), ())), preferred_element_type=f32)


def dot_t(a, b):
    return lax.dot_general(a, b, (((1,), (1,)), ((), ())), preferred_element_type=f32)


def split(x):
    hi = x.astype(bf16).astype(f32)
    return hi, x - hi


def call(body, out_shape, scratch=(), limit=32 * 2**20, cost=None):
    return pl.pallas_call(
        body,
        out_shape=out_shape,
        scratch_shapes=list(scratch),
        compiler_params=pltpu.CompilerParams(vmem_limit_bytes=limit),
    )


def attend(gathered, paged, fresh_keys, fresh_values, bias, fresh_bias, out, block):
    sent = jnp.concatenate([gathered[:, i, :].astype(f32) for i in range(STEPS)], axis=0)
    shape = (STEPS * GROUP * 4, WIDTH)
    quarter = iota(shape, 0) % 4
    diagonal = iota(shape, 1) // QUARTER == quarter
    turned = [sent] + [pltpu.roll(sent, QUARTER * d, 1) for d in range(1, 4)]
    pick_row = iota((GROUP * STEPS, shape[0]), 0)
    pick_col = iota((GROUP * STEPS, shape[0]), 1)
    pick = (pick_row // STEPS == (pick_col // 4) % GROUP) & (
        pick_row % STEPS == pick_col // (4 * GROUP)
    )
    pick = jnp.where(pick, 1.0, 0.0).astype(bf16)
    keys = paged[0, 0].reshape(-1, WIDTH)
    values = paged[1, 0].reshape(-1, WIDTH)
    fresh_k = fresh_keys[...]
    fresh_v = fresh_values[...]
    ones = jnp.ones((keys.shape[0], WIDTH), bf16)
    fresh_ones = jnp.ones((fresh_k.shape[0], WIDTH), bf16)
    scale = WIDTH ** (-0.5)
    lane = iota((GROUP * STEPS, WIDTH), 1)
    place = iota((GROUP * STEPS, WIDTH), 0) % 8
    stats = None
    for r in range(ROWS):
        chosen = turned[(3 - r) % 4]
        for c in range(3):
            chosen = jnp.where(quarter == c, turned[(c - r) % 4], chosen)
        chosen = jnp.where(diagonal, chosen, 0.0).astype(bf16)
        query = dot(pick, chosen).astype(bf16)
        scores = dot_t(query, keys) * scale + bias[r : r + 1, :]
        fresh = dot_t(query, fresh_k) * scale + fresh_bias[r]
        peak = jnp.maximum(
            jnp.max(scores, axis=1, keepdims=True), jnp.max(fresh, axis=1, keepdims=True)
        )
        peak = jnp.maximum(peak, floor).astype(bf16).astype(f32)
        weights = jnp.exp(scores - peak).astype(bf16)
        fresh_weights = jnp.exp(fresh - peak).astype(bf16)
        total = dot(weights, ones) + dot(fresh_weights, fresh_ones)
        summed = dot(weights, values) + dot(fresh_weights, fresh_v)
        mean = summed / jnp.where(total > 0.0, total, 1.0)
        block[:, 8 * r : 8 * r + 8, :] = mean.reshape(SIDE, 8, WIDTH)
        hi, rest = split(total)
        at = lane - place - 8 * r
        stat = jnp.where(at == 0, peak, jnp.where(at == 32, hi, jnp.where(at == 64, rest, 0.0)))
        stats = stat if stats is None else stats + stat
    stats = stats.reshape(SIDE, 8, WIDTH)
    block[:, 32:40, :] = jnp.broadcast_to(
        jnp.sum(stats, axis=1, keepdims=True), (SIDE, 8, WIDTH)
    )
    out[...] = block[...].astype(bf16)


def merged(got):
    parts = got[...].astype(f32)
    n = parts.shape[0]
    means, stats = parts[:, :32, :], parts[:, 32:40, :]
    stats = jnp.concatenate([stats] * 4, axis=1).reshape(n * 32, WIDTH)
    at = iota((n * 32, WIDTH), 1) - iota((n * 32, WIDTH), 0) % 32
    ones = jnp.ones((WIDTH, WIDTH), bf16)
    peaks = dot(jnp.where(at == 0, stats, 0.0).astype(bf16), ones).reshape(n, 32, WIDTH)
    totals = dot(jnp.where((at == 32) | (at == 64), stats, 0.0).astype(bf16), ones)
    totals = totals.reshape(n, 32, WIDTH)
    peak = jnp.max(peaks, axis=0)
    factors = jnp.exp(peaks - peak[None]) * totals
    total = jnp.sum(factors, axis=0)
    mean = jnp.sum(factors * means, axis=0) / jnp.where(total > 0.0, total, 1.0)
    return peak, total, mean


def join(got, out):
    peak, total, mean = merged(got)
    hi, rest = split(total)
    at = iota((32, WIDTH), 1) - iota((32, WIDTH), 0)
    stat = jnp.where(at == 0, peak, jnp.where(at == 32, hi, jnp.where(at == 64, rest, 0.0)))
    stat = jnp.broadcast_to(jnp.sum(stat, axis=0, keepdims=True), (8, WIDTH))
    block = jnp.concatenate([mean, stat], axis=0).astype(bf16)
    out[...] = jnp.broadcast_to(block[None], out.shape)


def finish(got, out):
    peak, total, mean = merged(got)
    to, of = iota((32, 32), 0), iota((32, 32), 1)
    move = (to // 16 == (of // 4) % 2) & ((to // 4) % 4 == of % 4) & (to % 4 == of // 8)
    moved = dot(jnp.where(move, 1.0, 0.0).astype(bf16), mean.astype(bf16)).astype(bf16)
    out[...] = jnp.broadcast_to(moved[None], out.shape)


def project(attended, weight, out):
    features = jnp.concatenate(
        [attended[i, COUNT * j : COUNT * (j + 1), :] for i in range(SIDE) for j in range(2)],
        axis=1,
    )
    out[...] = jnp.broadcast_to(dot(features, weight[...])[None], out.shape)


def normalise(parts, stream_in, gain, out, stream_out):
    stream = stream_in[...] + jnp.sum(parts[...], axis=0)
    for i in range(STEPS):
        stream_out[i] = stream[ROWS * i : ROWS * (i + 1)]
    squares = jnp.sum(stream * stream, axis=1, keepdims=True)
    hi, rest = split(squares)
    mid, rest = split(rest)
    at = iota((COUNT, WIDTH), 1) - iota((COUNT, WIDTH), 0)
    stat = jnp.where(at == 0, hi, jnp.where(at == 32, mid, jnp.where(at == 64, rest, 0.0)))
    stat = jnp.broadcast_to(jnp.sum(stat, axis=0, keepdims=True), (8, WIDTH))
    scaled = stream * gain[...]
    block = jnp.concatenate([scaled[:, :WIDTH], scaled[:, WIDTH:], stat], axis=0).astype(bf16)
    out[...] = jnp.broadcast_to(block[None], out.shape)


def feed(got, weight, out):
    n = got.shape[0]
    tokens = jnp.concatenate(
        [got[s, COUNT * j : COUNT * (j + 1), :] for s in range(n) for j in range(2)], axis=1
    )
    stats = jnp.sum(got[:, 32:40, :].astype(f32), axis=0)
    stats = jnp.concatenate([stats, stats], axis=0)
    at = iota((COUNT, WIDTH), 1) - iota((COUNT, WIDTH), 0)
    stats = jnp.where((at == 0) | (at == 32) | (at == 64), stats, 0.0)
    squares = jnp.sum(stats, axis=1, keepdims=True)
    inverse = lax.rsqrt(squares / (n * 2 * WIDTH) + epsilon)
    gate = dot_t(tokens, weight[0]) * inverse
    up = dot_t(tokens, weight[1]) * inverse
    hidden = gate / (1.0 + jnp.exp(-gate)) * up
    for i in range(STEPS):
        out[i] = hidden[ROWS * i : ROWS * (i + 1)].astype(bf16)


def send(x, axis):
    return lax.all_to_all(x, axis, split_axis=0, concat_axis=0, tiled=True)


def shards(
    queries,
    drafted_key_value,
    paged_key_value,
    block_table,
    page_count,
    tail_fill,
    out_weight,
    stream_in,
    norm_gain,
    gate_up,
):
    seq_index = lax.axis_index(("z", "y"))
    seq_count = lax.axis_size(("z", "y"))
    pages, page_len = paged_key_value.shape[2], paged_key_value.shape[3]
    columns = out_weight.shape[1]
    units = gate_up.shape[1]

    mine = queries.reshape(STEPS, ROWS * QUARTER)
    gathered = send(jnp.broadcast_to(mine[None], (seq_count, *mine.shape)), ("z", "y"))

    slots = seq_index * pages + jnp.arange(pages, dtype=jnp.int32)
    page_index = jnp.arange(block_table.shape[1], dtype=jnp.int32)
    held = (block_table[:, :, None] == slots[None, None, :]) & (
        page_index[None, :, None] < page_count[:, None, None]
    )
    last = page_index[None, :] == page_count[:, None] - 1
    fill = jnp.where(last, tail_fill[:, None], page_len)
    filled = jnp.max(jnp.where(held, fill[:, :, None], 0), axis=1)
    bias = jnp.where(jnp.arange(page_len)[None, None, :] < filled[:, :, None], 0.0, low)
    bias = bias.reshape(ROWS, pages * page_len).astype(f32)
    row = jnp.arange(ROWS)[:, None, None]
    step = (jnp.arange(GROUP * STEPS) % STEPS)[None, :, None]
    key = jnp.arange(COUNT)[None, None, :]
    ok = (key % ROWS == row) & (key // ROWS <= step) & (row == seq_index)
    fresh_bias = jnp.where(ok, 0.0, low).astype(f32)
    fresh_keys = drafted_key_value[:, :, 0, 0].reshape(COUNT, WIDTH)
    fresh_values = drafted_key_value[:, :, 1, 0].reshape(COUNT, WIDTH)

    shape = jax.ShapeDtypeStruct
    block = call(
        attend, shape((SIDE, 40, WIDTH), bf16), [pltpu.VMEM((SIDE, 40, WIDTH), f32)]
    )(gathered, paged_key_value, fresh_keys, fresh_values, bias, fresh_bias)
    block = call(join, shape((SIDE, 40, WIDTH), bf16))(send(block, "y"))
    attended = call(finish, shape((SIDE, 32, WIDTH), bf16))(send(block, "z"))
    partial_sum = call(project, shape((SIDE, COUNT, columns), f32))(
        send(attended, "y"), out_weight
    )
    scaled, stream = call(
        normalise,
        (shape((SIDE, 40, WIDTH), bf16), shape((STEPS, ROWS, columns), f32)),
    )(
        send(partial_sum, ("x", "core")),
        stream_in.reshape(COUNT, columns),
        norm_gain.reshape(1, columns),
    )
    scaled = lax.all_gather(send(scaled, "y"), "z").reshape(seq_count, 40, WIDTH)
    hidden = call(feed, shape((STEPS, ROWS, units), bf16))(scaled, gate_up)
    return hidden, stream


def solution(mesh):
    fine = Mesh(mesh.devices.reshape(4, 2, 8, 8), ("x", "core", "z", "y"))
    kvh, seq = ("x", "core"), ("z", "y")
    placed = (
        P(None, None, kvh + seq),
        P(None, None, None, kvh, None),
        P(None, kvh, seq, None, None),
        P(),
        P(),
        P(),
        P(kvh, seq),
        P(None, None, seq),
        P(seq),
        P(None, kvh + seq, None),
    )
    return jax.shard_map(
        shards,
        mesh=fine,
        in_specs=placed,
        out_specs=(P(None, None, kvh + seq), P(None, None, seq)),
        check_vma=False,
    )
```

time: 409 us -> 123 us (0.30)
  the two profiles are of different devices: /device:TPU:56 before, /device:TPU:8 now
where the time goes in v1:
time: 123 us; the launch traced here: 122 us
  blocking collectives  58.5 us (48%)
  starting transfers between devices  25.6 us (21%)
  waiting for transfers between devices  14 us (11%)
  local copies, waits for them, and re-layouts  13.7 us (11%)
  Pallas kernels  6.34 us (5%)
  other arithmetic  3.21 us (3%)
    all_to_all x3, blocking collectives, send(): return lax.all_to_all(x, axis, split_axis=0, concat_axis=0, tiled=True)  32.8 us
    all_gather x1, blocking collectives, shards(): lax.all_gather(send(scaled, 'y'), 'z').reshape(seq_count, 40, WIDTH)  25.7 us
    all_to_all x3, starting transfers between devices, send(): return lax.all_to_all(x, axis, split_axis=0, concat_axis=0, tiled=True)  25.6 us
    all_to_all x3, waiting for transfers between devices, send(): return lax.all_to_all(x, axis, split_axis=0, concat_axis=0, tiled=True)  14 us
    unnamed x12, local copies, waits for them, and re-layouts  10.7 us
  transfers between devices with their start and end apart: 3, of which 3 were waited for; matrix products, arithmetic and copies ran while one was open for 9% of the time, Pallas kernels for 0%

profile of v1, /device:TPU:8, one launch (start us, length us, event | category | flops | bytes accessed | tf_op | source)
XLA Modules:
  0.0 122.0 jit_solution(4667085756186016864)
XLA Ops:
  0.6 0.8 broadcast_in_dim.60
  1.4 0.6 broadcast_in_dim.61
  2.0 16.6 %all-to-all-start = ((bf16[64,4,128]{2,1,0:T(4,128)(2,1)}), bf16[64,4,128]{2,1,0:T(4,128)(2,1)S(1)}, u32[]{:S(2)}, u32[]{:S(2)}) async-start(bf16[64,4,128]{2,1,0:T(4,128)(2,1)} %broadcast_in_dim.61), calls=%async_computation | async-start | bytes 131072 | tf_op jit(solution)/shard_map/all_to_all | solution.py:180
  18.6 0.7 broadcast_add_fusion
  19.3 0.7 iota_compare_fusion.2
  20.1 0.7 fusion.1
  20.8 0.9 select_reduce_fusion
  21.7 0.1 broadcast_bitcast_fusion
  21.8 0.8 fusion.2
  22.6 0.1 broadcast_compare_fusion
  22.7 0.1 and_select_fusion.fresh_bias
  22.8 7.2 %all-to-all-done.gathered = bf16[64,4,128]{2,1,0:T(4,128)(2,1)S(1)} async-done(((bf16[64,4,128]{2,1,0:T(4,128)(2,1)}), bf16[64,4,128]{2,1,0:T(4,128)(2,1)S(1)}, u32[]{:S(2)}, u32[]{:S(2)}) %all-to-all-start) | async-done | bytes 65568 | tf_op jit(solution)/shard_map/all_to_all | solution.py:180
  30.0 1.0 copy-done.2
  31.1 2.3 %shard_map.113 = bf16[8,40,128]{2,1,0:T(8,128)(2,1)S(1)} custom-call(bf16[64,4,128]{2,1,0:T(4,128)(2,1)S(1)} %all-to-all-done.gathered, bf16[2,1,8,128,128]{4,3,2,1,0:T(8,128)(2,1)S(1)} %copy-done.2, bf16[16,128]{1,0:T(8,128)(2,1)S(1)} %bitcast.12, bf16[16,128]{1,0:T(8,128)(2,1)S(1)} %bitcast.11, f32[4,1024]{1,0:T(4,128)S(1)} %fusion.bias, ...), custom_call_target="tpu_custom_call" | custom-call | tf_op jit(solution)/shard_map/pallas_call | solution.py:223
  33.4 10.8 %all_to_all.30.got = bf16[8,40,128]{2,1,0:T(8,128)(2,1)S(1)} all-to-all(bf16[8,40,128]{2,1,0:T(8,128)(2,1)S(1)} %shard_map.113), channel_id=1, replica_groups=mesh['x'=4,'core'=2,'z'=8,'y'=8] {'y'}, dimensions={0} | all-to-all | bytes 163840 | tf_op jit(solution)/shard_map/all_to_all | solution.py:180
  44.2 0.2 shard_map.114
  44.4 11.2 %all_to_all.31.got = bf16[8,40,128]{2,1,0:T(8,128)(2,1)S(1)} all-to-all(bf16[8,40,128]{2,1,0:T(8,128)(2,1)S(1)} %shard_map.114), channel_id=1, replica_groups=mesh['x'=4,'core'=2,'z'=8,'y'=8] {'z'}, dimensions={0} | all-to-all | bytes 163840 | tf_op jit(solution)/shard_map/all_to_all | solution.py:180
  55.6 0.3 shard_map.115
  56.0 10.8 %all_to_all.32.attended = bf16[8,32,128]{2,1,0:T(8,128)(2,1)S(1)} all-to-all(bf16[8,32,128]{2,1,0:T(8,128)(2,1)S(1)} %shard_map.115), channel_id=1, replica_groups=mesh['x'=4,'core'=2,'z'=8,'y'=8] {'y'}, dimensions={0} | all-to-all | bytes 131072 | tf_op jit(solution)/shard_map/all_to_all | solution.py:180
  66.7 1.2 %copy-done.1 = bf16[2048,256]{1,0:T(8,128)(2,1)S(1)} copy-done((bf16[2048,256]{1,0:T(8,128)(2,1)S(1)}, bf16[2048,256]{1,0:T(8,128)(2,1)}, u32[]{:S(2)}) %copy-start.1) | copy-done | bytes 1048600
  68.0 0.9 shard_map.116
  68.9 4.3 %all-to-all-start.4 = ((f32[8,16,256]{2,1,0:T(8,128)}), f32[8,16,256]{2,1,0:T(8,128)S(1)}, u32[]{:S(2)}, u32[]{:S(2)}) async-start(f32[8,16,256]{2,1,0:T(8,128)} %shard_map.116), calls=%async_computation.4 | async-start | bytes 262144 | tf_op jit(solution)/shard_map/all_to_all | solution.py:180
  73.2 0.7 reshape.206.stream_in
  73.9 5.4 %all-to-all-done.4.parts = f32[8,16,256]{2,1,0:T(8,128)S(1)} async-done(((f32[8,16,256]{2,1,0:T(8,128)}), f32[8,16,256]{2,1,0:T(8,128)S(1)}, u32[]{:S(2)}, u32[]{:S(2)}) %all-to-all-start.4) | async-done | bytes 131104 | tf_op jit(solution)/shard_map/all_to_all | solution.py:180
  79.3 0.7 copy-done.3
  80.0 0.7 shard_map.117
  80.7 4.7 %all-to-all-start.5 = ((bf16[8,40,128]{2,1,0:T(8,128)(2,1)}), bf16[8,40,128]{2,1,0:T(8,128)(2,1)S(1)}, u32[]{:S(2)}, u32[]{:S(2)}) async-start(bf16[8,40,128]{2,1,0:T(8,128)(2,1)} %get-tuple-element.4), calls=%async_computation.5 | async-start | bytes 163840 | tf_op jit(solution)/shard_map/all_to_all | solution.py:180
  85.4 5.7 %copy.15.weight = bf16[2,52,16384]{2,1,0:T(8,128)(2,1)} copy(bf16[2,52,16384]{2,0,1:T(2,128)(2,1)} %param.19) | data formatting | bytes 6815744 | tf_op args[9]
  91.1 1.3 %all-to-all-done.5 = bf16[8,40,128]{2,1,0:T(8,128)(2,1)S(1)} async-done(((bf16[8,40,128]{2,1,0:T(8,128)(2,1)}), bf16[8,40,128]{2,1,0:T(8,128)(2,1)S(1)}, u32[]{:S(2)}, u32[]{:S(2)}) %all-to-all-start.5) | async-done | bytes 81952 | tf_op jit(solution)/shard_map/all_to_all | solution.py:180
  92.4 25.7 %all-gather.got = bf16[64,40,128]{2,1,0:T(8,128)(2,1)S(1)} all-gather(bf16[8,40,128]{2,1,0:T(8,128)(2,1)S(1)} %all-to-all-done.5), channel_id=2, replica_groups=mesh['x'=4,'core'=2,'z'=8,'y'=8] {'z'}, dimensions={0}, use_global_device_ids=true | all-gather | bytes 737280 | tf_op jit(solution)/shard_map/all_gather | solution.py:239
  118.1 2.0 %copy-done = bf16[2,52,16384]{2,1,0:T(8,128)(2,1)S(1)} copy-done((bf16[2,52,16384]{2,1,0:T(8,128)(2,1)S(1)}, bf16[2,52,16384]{2,1,0:T(8,128)(2,1)}, u32[]{:S(2)}) %copy-start) | copy-done | bytes 3407896
  120.2 1.8 %shard_map.118 = bf16[4,4,52]{2,1,0:T(4,128)(2,1)} custom-call(bf16[64,40,128]{2,1,0:T(8,128)(2,1)S(1)} %all-gather.got, bf16[2,52,16384]{2,1,0:T(8,128)(2,1)S(1)} %copy-done), custom_call_target="tpu_custom_call" | custom-call | tf_op jit(solution)/shard_map/pallas_call | solution.py:240
  (14 shorter events, 0.1 us)
Async XLA Ops:
  2.0 28.0 %all-to-all-start = ((bf16[64,4,128]{2,1,0:T(4,128)(2,1)}), bf16[64,4,128]{2,1,0:T(4,128)(2,1)S(1)}, u32[]{:S(2)}, u32[]{:S(2)}) async-start(bf16[64,4,128]{2,1,0:T(4,128)(2,1)} %broadcast_in_dim.61), calls=%async_computation | async-start | bytes 131072 | tf_op jit(solution)/shard_map/all_to_all | solution.py:180
  30.0 1.0 copy-start.2
  66.7 1.2 %copy-start.1 = (bf16[2048,256]{1,0:T(8,128)(2,1)S(1)}, bf16[2048,256]{1,0:T(8,128)(2,1)}, u32[]{:S(2)}) copy-start(bf16[2048,256]{1,0:T(8,128)(2,1)} %weight.2) | copy-start | bytes 3145732
  68.9 10.4 %all-to-all-start.4 = ((f32[8,16,256]{2,1,0:T(8,128)}), f32[8,16,256]{2,1,0:T(8,128)S(1)}, u32[]{:S(2)}, u32[]{:S(2)}) async-start(f32[8,16,256]{2,1,0:T(8,128)} %shard_map.116), calls=%async_computation.4 | async-start | bytes 262144 | tf_op jit(solution)/shard_map/all_to_all | solution.py:180
  79.3 0.7 copy-start.3
  80.7 11.7 %all-to-all-start.5 = ((bf16[8,40,128]{2,1,0:T(8,128)(2,1)}), bf16[8,40,128]{2,1,0:T(8,128)(2,1)S(1)}, u32[]{:S(2)}, u32[]{:S(2)}) async-start(bf16[8,40,128]{2,1,0:T(8,128)(2,1)} %get-tuple-element.4), calls=%async_computation.5 | async-start | bytes 163840 | tf_op jit(solution)/shard_map/all_to_all | solution.py:180
  118.1 2.0 %copy-start = (bf16[2,52,16384]{2,1,0:T(8,128)(2,1)S(1)}, bf16[2,52,16384]{2,1,0:T(8,128)(2,1)}, u32[]{:S(2)}) copy-start(bf16[2,52,16384]{2,1,0:T(8,128)(2,1)} %copy.15.weight) | copy-start | bytes 10223620

commit v2 on v1

--- a/solution.py
+++ b/solution.py
@@ -47,6 +47,21 @@
         scratch_shapes=list(scratch),
         compiler_params=pltpu.CompilerParams(vmem_limit_bytes=limit),
     )
+
+
+def copies(queries, out):
+    x = queries[...].astype(f32)
+    x = jnp.concatenate([x[:, r, :] for r in range(ROWS)], axis=1).astype(bf16)
+    out[...] = jnp.broadcast_to(x[None], out.shape)
+
+
+def fetch(*refs):
+    n = len(refs) // 2
+    moves = [pltpu.make_async_copy(refs[i], refs[n + i], refs[-1].at[i]) for i in range(n)]
+    for move in moves:
+        move.start()
+    for move in moves:
+        move.wait()
 
 
 def attend(gathered, paged, fresh_keys, fresh_values, bias, fresh_bias, out, block):
@@ -198,8 +213,17 @@
     columns = out_weight.shape[1]
     units = gate_up.shape[1]
 
-    mine = queries.reshape(STEPS, ROWS * QUARTER)
-    gathered = send(jnp.broadcast_to(mine[None], (seq_count, *mine.shape)), ("z", "y"))
+    shape = jax.ShapeDtypeStruct
+    mine = call(copies, shape((seq_count, STEPS, ROWS * QUARTER), bf16))(queries)
+    gathered = send(mine, ("z", "y"))
+    held = (paged_key_value, out_weight)
+    paged_key_value, out_weight = pl.pallas_call(
+        fetch,
+        in_specs=[pl.BlockSpec(memory_space=pl.ANY)] * len(held),
+        out_specs=[pl.BlockSpec(memory_space=pltpu.VMEM)] * len(held),
+        out_shape=[shape(x.shape, x.dtype) for x in held],
+        scratch_shapes=[pltpu.SemaphoreType.DMA((len(held),))],
+    )(*held)
 
     slots = seq_index * pages + jnp.arange(pages, dtype=jnp.int32)
     page_index = jnp.arange(block_table.shape[1], dtype=jnp.int32)
@@ -219,7 +243,6 @@
     fresh_keys = drafted_key_value[:, :, 0, 0].reshape(COUNT, WIDTH)
     fresh_values = drafted_key_value[:, :, 1, 0].reshape(COUNT, WIDTH)
 
-    shape = jax.ShapeDtypeStruct
     block = call(
         attend, shape((SIDE, 40, WIDTH), bf16), [pltpu.VMEM((SIDE, 40, WIDTH), f32)]
     )(gathered, paged_key_value, fresh_keys, fresh_values, bias, fresh_bias)
@@ -230,14 +253,13 @@
     )
     scaled, stream = call(
         normalise,
-        (shape((SIDE, 40, WIDTH), bf16), shape((STEPS, ROWS, columns), f32)),
+        (shape((seq_count, 40, WIDTH), bf16), shape((STEPS, ROWS, columns), f32)),
     )(
         send(partial_sum, ("x", "core")),
         stream_in.reshape(COUNT, columns),
         norm_gain.reshape(1, columns),
     )
-    scaled = lax.all_gather(send(scaled, "y"), "z").reshape(seq_count, 40, WIDTH)
-    hidden = call(feed, shape((STEPS, ROWS, units), bf16))(scaled, gate_up)
+    hidden = call(feed, shape((STEPS, ROWS, units), bf16))(send(scaled, ("z", "y")), gate_up)
     return hidden, stream
 
 

time: 123 us -> 115 us (0.935)
  blocking collectives: 58.5 us -> 35.3 us
  waiting for transfers between devices: 14 us -> 27.1 us
  Pallas kernels: 6.34 us -> 9.86 us
  local copies, waits for them, and re-layouts: 13.7 us -> 11.5 us
    all_gather x1 -> x0, blocking collectives: 25.7 us -> none  [shards(): lax.all_gather(send(scaled, 'y'), 'z').reshape(seq_count, 40, WIDTH)]
    all_to_all x3, waiting for transfers between devices: 14 us -> 27.1 us  [send(): return lax.all_to_all(x, axis, split_axis=0, concat_axis=0, tiled=True)]
    pallas_call x2 -> x4, Pallas kernels: 2.54 us -> 6.04 us  [the longest x1 2.56 us: shards(): pl.pallas_call(fetch, in_specs=[pl.BlockSpec(memory_space=pl.ANY)] * len(...]
    all_to_all x3, blocking collectives: 32.8 us -> 35.3 us  [send(): return lax.all_to_all(x, axis, split_axis=0, concat_axis=0, tiled=True)]
    broadcast_in_dim x2 -> x0, local copies, waits for them, and re-layouts: 1.41 us -> none  [shards(): jnp.broadcast_to(mine[None], (seq_count, *mine.shape))]
    unnamed x12 -> x16, local copies, waits for them, and re-layouts: 10.7 us -> 10.7 us
  transfers between devices with their start and end apart: 3 -> 3, of which waited for: 3 -> 3; matrix products, arithmetic and copies ran while one was open for 9% -> 9% of each run, Pallas kernels for 0% -> 2%
where the time goes in v2:
time: 115 us; the launch traced here: 114 us
  blocking collectives  35.3 us (31%)
  waiting for transfers between devices  27.1 us (24%)
  starting transfers between devices  26.4 us (23%)
  local copies, waits for them, and re-layouts  11.5 us (10%)
  Pallas kernels  9.86 us (9%)
  other arithmetic  3.21 us (3%)
    all_to_all x3, blocking collectives, send(): return lax.all_to_all(x, axis, split_axis=0, concat_axis=0, tiled=True)  35.3 us
    all_to_all x3, waiting for transfers between devices, send(): return lax.all_to_all(x, axis, split_axis=0, concat_axis=0, tiled=True)  27.1 us
    all_to_all x3, starting transfers between devices, send(): return lax.all_to_all(x, axis, split_axis=0, concat_axis=0, tiled=True)  26.4 us
    unnamed x16, local copies, waits for them, and re-layouts  10.7 us
    pallas_call x1, Pallas kernels, shards(): pl.pallas_call(fetch, in_specs=[pl.BlockSpec(memory_space=pl.ANY)] * len(...  2.56 us
    pallas_call x1, Pallas kernels, shards(): call(attend, shape((SIDE, 40, WIDTH), bf16), [pltpu.VMEM((SIDE, 40, WIDTH...  2.35 us
  transfers between devices with their start and end apart: 3, of which 3 were waited for; matrix products, arithmetic and copies ran while one was open for 9% of the time, Pallas kernels for 2%

profile of v2, /device:TPU:8, one launch (start us, length us, event | category | flops | bytes accessed | tf_op | source)
XLA Modules:
  0.0 114.2 jit_solution(5860686938430226924)
XLA Ops:
  0.6 0.0 copy-start.3
  0.6 0.7 copy-done.3
  1.3 0.7 shard_map.113
  2.0 16.6 %all-to-all-start = ((bf16[64,4,128]{2,1,0:T(4,128)(2,1)}), bf16[64,4,128]{2,1,0:T(4,128)(2,1)S(1)}, u32[]{:S(2)}, u32[]{:S(2)}) async-start(bf16[64,4,128]{2,1,0:T(4,128)(2,1)} %shard_map.113), calls=%async_computation | async-start | bytes 131072 | tf_op jit(solution)/shard_map/all_to_all | solution.py:195
  18.6 0.7 broadcast_add_fusion
  19.3 0.7 iota_compare_fusion.2
  20.1 0.7 fusion.1
  20.8 0.9 select_reduce_fusion
  21.7 0.1 broadcast_bitcast_fusion
  21.8 0.8 fusion.2
  22.6 0.1 broadcast_compare_fusion
  22.7 2.6 %shard_map.114 = (bf16[2,1,8,128,128]{4,3,2,1,0:T(8,128)(2,1)}, bf16[2048,256]{1,0:T(8,128)(2,1)}) custom-call(bf16[2,1,8,128,128]{4,3,2,1,0:T(8,128)(2,1)} %refs_0_.1, bf16[2048,256]{1,0:T(8,128)(2,1)} %refs_1_.1), custom_call_target="tpu_custom_call" | custom-call | tf_op jit(solution)/shard_map/pallas_call | solution.py:220
  25.2 0.1 and_select_fusion.fresh_bias
  25.4 4.7 %all-to-all-done.gathered = bf16[64,4,128]{2,1,0:T(4,128)(2,1)S(1)} async-done(((bf16[64,4,128]{2,1,0:T(4,128)(2,1)}), bf16[64,4,128]{2,1,0:T(4,128)(2,1)S(1)}, u32[]{:S(2)}, u32[]{:S(2)}) %all-to-all-start) | async-done | bytes 65568 | tf_op jit(solution)/shard_map/all_to_all | solution.py:195
  30.0 1.0 copy-done.2
  31.1 2.4 %shard_map.115 = bf16[8,40,128]{2,1,0:T(8,128)(2,1)S(1)} custom-call(bf16[64,4,128]{2,1,0:T(4,128)(2,1)S(1)} %all-to-all-done.gathered, bf16[2,1,8,128,128]{4,3,2,1,0:T(8,128)(2,1)S(1)} %copy-done.2, bf16[16,128]{1,0:T(8,128)(2,1)S(1)} %bitcast.12, bf16[16,128]{1,0:T(8,128)(2,1)S(1)} %bitcast.11, f32[4,1024]{1,0:T(4,128)S(1)} %fusion.bias, ...), custom_call_target="tpu_custom_call" | custom-call | tf_op jit(solution)/shard_map/pallas_call | solution.py:246
  33.4 10.8 %all_to_all.30.got = bf16[8,40,128]{2,1,0:T(8,128)(2,1)S(1)} all-to-all(bf16[8,40,128]{2,1,0:T(8,128)(2,1)S(1)} %shard_map.115), channel_id=1, replica_groups=mesh['x'=4,'core'=2,'z'=8,'y'=8] {'y'}, dimensions={0} | all-to-all | bytes 163840 | tf_op jit(solution)/shard_map/all_to_all | solution.py:195
  44.2 0.2 shard_map.116
  44.4 13.8 %all_to_all.31.got = bf16[8,40,128]{2,1,0:T(8,128)(2,1)S(1)} all-to-all(bf16[8,40,128]{2,1,0:T(8,128)(2,1)S(1)} %shard_map.116), channel_id=1, replica_groups=mesh['x'=4,'core'=2,'z'=8,'y'=8] {'z'}, dimensions={0} | all-to-all | bytes 163840 | tf_op jit(solution)/shard_map/all_to_all | solution.py:195
  58.2 0.3 shard_map.117
  58.5 10.8 %all_to_all.32.attended = bf16[8,32,128]{2,1,0:T(8,128)(2,1)S(1)} all-to-all(bf16[8,32,128]{2,1,0:T(8,128)(2,1)S(1)} %shard_map.117), channel_id=1, replica_groups=mesh['x'=4,'core'=2,'z'=8,'y'=8] {'y'}, dimensions={0} | all-to-all | bytes 131072 | tf_op jit(solution)/shard_map/all_to_all | solution.py:195
  69.3 1.2 %copy-done.1 = bf16[2048,256]{1,0:T(8,128)(2,1)S(1)} copy-done((bf16[2048,256]{1,0:T(8,128)(2,1)S(1)}, bf16[2048,256]{1,0:T(8,128)(2,1)}, u32[]{:S(2)}) %copy-start.1) | copy-done | bytes 1048600
  70.5 0.9 shard_map.118
  71.4 4.3 %all-to-all-start.4 = ((f32[8,16,256]{2,1,0:T(8,128)}), f32[8,16,256]{2,1,0:T(8,128)S(1)}, u32[]{:S(2)}, u32[]{:S(2)}) async-start(f32[8,16,256]{2,1,0:T(8,128)} %shard_map.118), calls=%async_computation.4 | async-start | bytes 262144 | tf_op jit(solution)/shard_map/all_to_all | solution.py:195
  75.7 0.0 copy-done.5
  75.8 6.1 %all-to-all-done.4.parts = f32[8,16,256]{2,1,0:T(8,128)S(1)} async-done(((f32[8,16,256]{2,1,0:T(8,128)}), f32[8,16,256]{2,1,0:T(8,128)S(1)}, u32[]{:S(2)}, u32[]{:S(2)}) %all-to-all-start.4) | async-done | bytes 131104 | tf_op jit(solution)/shard_map/all_to_all | solution.py:195
  81.9 1.0 shard_map.119
  82.8 5.5 %all-to-all-start.5 = ((bf16[64,40,128]{2,1,0:T(8,128)(2,1)}), bf16[64,40,128]{2,1,0:T(8,128)(2,1)S(1)}, u32[]{:S(2)}, u32[]{:S(2)}) async-start(bf16[64,40,128]{2,1,0:T(8,128)(2,1)} %get-tuple-element.8), calls=%async_computation.5 | async-start | bytes 1310720 | tf_op jit(solution)/shard_map/all_to_all | solution.py:195
  88.4 5.7 %copy.14.weight = bf16[2,52,16384]{2,1,0:T(8,128)(2,1)} copy(bf16[2,52,16384]{2,0,1:T(2,128)(2,1)} %param.19) | data formatting | bytes 6815744 | tf_op args[9]
  94.0 16.3 %all-to-all-done.5.got = bf16[64,40,128]{2,1,0:T(8,128)(2,1)S(1)} async-done(((bf16[64,40,128]{2,1,0:T(8,128)(2,1)}), bf16[64,40,128]{2,1,0:T(8,128)(2,1)S(1)}, u32[]{:S(2)}, u32[]{:S(2)}) %all-to-all-start.5) | async-done | bytes 655392 | tf_op jit(solution)/shard_map/all_to_all | solution.py:195
  110.4 2.0 %copy-done = bf16[2,52,16384]{2,1,0:T(8,128)(2,1)S(1)} copy-done((bf16[2,52,16384]{2,1,0:T(8,128)(2,1)S(1)}, bf16[2,52,16384]{2,1,0:T(8,128)(2,1)}, u32[]{:S(2)}) %copy-start) | copy-done | bytes 3407896
  112.4 1.8 %shard_map.120 = bf16[4,4,52]{2,1,0:T(4,128)(2,1)} custom-call(bf16[64,40,128]{2,1,0:T(8,128)(2,1)S(1)} %all-to-all-done.5.got, bf16[2,52,16384]{2,1,0:T(8,128)(2,1)S(1)} %copy-done), custom_call_target="tpu_custom_call" | custom-call | tf_op jit(solution)/shard_map/pallas_call | solution.py:262
  (17 shorter events, 0.1 us)
Async XLA Ops:
  0.6 0.7 copy-start.3
  1.3 74.4 %copy-start.5 = (f32[4,4,256]{2,1,0:T(4,128)S(1)}, f32[4,4,256]{2,1,0:T(4,128)}, u32[]{:S(2)}) copy-start(f32[4,4,256]{2,1,0:T(4,128)} %param.17) | copy-start | bytes 49156
  1.3 80.6 %copy-start.4 = (f32[256]{0:T(256)S(1)}, f32[256]{0:T(256)}, u32[]{:S(2)}) copy-start(f32[256]{0:T(256)} %param.18) | copy-start | bytes 3076
  2.0 28.0 %all-to-all-start = ((bf16[64,4,128]{2,1,0:T(4,128)(2,1)}), bf16[64,4,128]{2,1,0:T(4,128)(2,1)S(1)}, u32[]{:S(2)}, u32[]{:S(2)}) async-start(bf16[64,4,128]{2,1,0:T(4,128)(2,1)} %shard_map.113), calls=%async_computation | async-start | bytes 131072 | tf_op jit(solution)/shard_map/all_to_all | solution.py:195
  30.0 1.0 copy-start.2
  69.3 1.2 %copy-start.1 = (bf16[2048,256]{1,0:T(8,128)(2,1)S(1)}, bf16[2048,256]{1,0:T(8,128)(2,1)}, u32[]{:S(2)}) copy-start(bf16[2048,256]{1,0:T(8,128)(2,1)} %get-tuple-element.7.weight) | copy-start | bytes 3145732
  71.4 10.4 %all-to-all-start.4 = ((f32[8,16,256]{2,1,0:T(8,128)}), f32[8,16,256]{2,1,0:T(8,128)S(1)}, u32[]{:S(2)}, u32[]{:S(2)}) async-start(f32[8,16,256]{2,1,0:T(8,128)} %shard_map.118), calls=%async_computation.4 | async-start | bytes 262144 | tf_op jit(solution)/shard_map/all_to_all | solution.py:195
  82.8 27.5 %all-to-all-start.5 = ((bf16[64,40,128]{2,1,0:T(8,128)(2,1)}), bf16[64,40,128]{2,1,0:T(8,128)(2,1)S(1)}, u32[]{:S(2)}, u32[]{:S(2)}) async-start(bf16[64,40,128]{2,1,0:T(8,128)(2,1)} %get-tuple-element.8), calls=%async_computation.5 | async-start | bytes 1310720 | tf_op jit(solution)/shard_map/all_to_all | solution.py:195
  110.4 2.0 %copy-start = (bf16[2,52,16384]{2,1,0:T(8,128)(2,1)S(1)}, bf16[2,52,16384]{2,1,0:T(8,128)(2,1)}, u32[]{:S(2)}) copy-start(bf16[2,52,16384]{2,1,0:T(8,128)(2,1)} %copy.14.weight) | copy-start | bytes 10223620

commit v3 on v1

--- a/solution.py
+++ b/solution.py
@@ -40,16 +40,76 @@
     return hi, x - hi
 
 
-def call(body, out_shape, scratch=(), limit=32 * 2**20, cost=None):
+def call(body, out_shape, inputs="", scratch=(), limit=32 * 2**20):
+    spaces = {"v": pltpu.VMEM, "h": pl.ANY, "s": pltpu.SMEM}
     return pl.pallas_call(
         body,
         out_shape=out_shape,
+        in_specs=[pl.BlockSpec(memory_space=spaces[c]) for c in inputs],
         scratch_shapes=list(scratch),
         compiler_params=pltpu.CompilerParams(vmem_limit_bytes=limit),
     )
 
 
-def attend(gathered, paged, fresh_keys, fresh_values, bias, fresh_bias, out, block):
+def begin(pairs, sems):
+    moves = [pltpu.make_async_copy(a, b, sems.at[i]) for i, (a, b) in enumerate(pairs)]
+    for move in moves:
+        move.start()
+    return moves
+
+
+def copies(queries, out):
+    x = queries[...].astype(f32)
+    x = jnp.concatenate([x[:, r, :] for r in range(ROWS)], axis=1).astype(bf16)
+    out[...] = jnp.broadcast_to(x[None], out.shape)
+
+
+def prepare(
+    table, count, tail, index, drafted, paged, bias, fresh_bias, fresh_keys, fresh_values, held, sems
+):
+    moves = begin([(paged, held)], sems)
+    pages, page_len = paged.shape[2], paged.shape[3]
+    row, page = iota(table.shape, 0), iota(table.shape, 1)
+    counts = tails = jnp.zeros(table.shape, jnp.int32)
+    for r in range(ROWS):
+        counts = jnp.where(row == r, count[r], counts)
+        tails = jnp.where(row == r, tail[r], tails)
+    fill = jnp.where(page == counts - 1, tails, page_len).astype(f32)
+    fill = jnp.where(page < counts, fill, 0.0)
+    slots = table[...]
+    token = iota((ROWS, page_len), 1).astype(f32)
+    for p in range(pages):
+        filled = jnp.where(slots == index[0] * pages + p, fill, 0.0)
+        filled = jnp.max(filled, axis=1, keepdims=True)
+        bias[:, p * page_len : (p + 1) * page_len] = jnp.where(token < filled, 0.0, low)
+    step = iota((GROUP * STEPS, COUNT), 0) % STEPS
+    key = iota((GROUP * STEPS, COUNT), 1)
+    causal = key // ROWS <= step
+    for r in range(ROWS):
+        ok = causal & (key % ROWS == r) & (index[0] == r)
+        fresh_bias[r] = jnp.where(ok, 0.0, low)
+    both = drafted[...].astype(f32)
+    fresh_keys[...] = both[:, 0, :].astype(bf16)
+    fresh_values[...] = both[:, 1, :].astype(bf16)
+    moves[0].wait()
+
+
+def attend(
+    gathered,
+    paged,
+    fresh_keys,
+    fresh_values,
+    bias,
+    fresh_bias,
+    out_weight,
+    gate_up,
+    out,
+    out_weight_held,
+    gate_up_held,
+    block,
+    sems,
+):
+    moves = begin([(out_weight, out_weight_held), (gate_up, gate_up_held)], sems)
     sent = jnp.concatenate([gathered[:, i, :].astype(f32) for i in range(STEPS)], axis=0)
     shape = (STEPS * GROUP * 4, WIDTH)
     quarter = iota(shape, 0) % 4
@@ -98,6 +158,8 @@
         jnp.sum(stats, axis=1, keepdims=True), (SIDE, 8, WIDTH)
     )
     out[...] = block[...].astype(bf16)
+    for move in moves:
+        move.wait()
 
 
 def merged(got):
@@ -140,11 +202,13 @@
         [attended[i, COUNT * j : COUNT * (j + 1), :] for i in range(SIDE) for j in range(2)],
         axis=1,
     )
-    out[...] = jnp.broadcast_to(dot(features, weight[...])[None], out.shape)
-
-
-def normalise(parts, stream_in, gain, out, stream_out):
-    stream = stream_in[...] + jnp.sum(parts[...], axis=0)
+    out[...] = jnp.broadcast_to(dot(features, weight[...]).astype(bf16)[None], out.shape)
+
+
+def normalise(parts, stream_in, gain, out, stream_out, rows):
+    for i in range(STEPS):
+        rows[ROWS * i : ROWS * (i + 1), :] = stream_in[i]
+    stream = rows[...] + jnp.sum(parts[...].astype(f32), axis=0)
     for i in range(STEPS):
         stream_out[i] = stream[ROWS * i : ROWS * (i + 1)]
     squares = jnp.sum(stream * stream, axis=1, keepdims=True)
@@ -198,46 +262,49 @@
     columns = out_weight.shape[1]
     units = gate_up.shape[1]
 
-    mine = queries.reshape(STEPS, ROWS * QUARTER)
-    gathered = send(jnp.broadcast_to(mine[None], (seq_count, *mine.shape)), ("z", "y"))
-
-    slots = seq_index * pages + jnp.arange(pages, dtype=jnp.int32)
-    page_index = jnp.arange(block_table.shape[1], dtype=jnp.int32)
-    held = (block_table[:, :, None] == slots[None, None, :]) & (
-        page_index[None, :, None] < page_count[:, None, None]
-    )
-    last = page_index[None, :] == page_count[:, None] - 1
-    fill = jnp.where(last, tail_fill[:, None], page_len)
-    filled = jnp.max(jnp.where(held, fill[:, :, None], 0), axis=1)
-    bias = jnp.where(jnp.arange(page_len)[None, None, :] < filled[:, :, None], 0.0, low)
-    bias = bias.reshape(ROWS, pages * page_len).astype(f32)
-    row = jnp.arange(ROWS)[:, None, None]
-    step = (jnp.arange(GROUP * STEPS) % STEPS)[None, :, None]
-    key = jnp.arange(COUNT)[None, None, :]
-    ok = (key % ROWS == row) & (key // ROWS <= step) & (row == seq_index)
-    fresh_bias = jnp.where(ok, 0.0, low).astype(f32)
-    fresh_keys = drafted_key_value[:, :, 0, 0].reshape(COUNT, WIDTH)
-    fresh_values = drafted_key_value[:, :, 1, 0].reshape(COUNT, WIDTH)
-
     shape = jax.ShapeDtypeStruct
-    block = call(
-        attend, shape((SIDE, 40, WIDTH), bf16), [pltpu.VMEM((SIDE, 40, WIDTH), f32)]
-    )(gathered, paged_key_value, fresh_keys, fresh_values, bias, fresh_bias)
-    block = call(join, shape((SIDE, 40, WIDTH), bf16))(send(block, "y"))
-    attended = call(finish, shape((SIDE, 32, WIDTH), bf16))(send(block, "z"))
-    partial_sum = call(project, shape((SIDE, COUNT, columns), f32))(
-        send(attended, "y"), out_weight
+    dma = pltpu.SemaphoreType.DMA
+    mine = call(copies, shape((seq_count, STEPS, ROWS * QUARTER), bf16), "v")(queries)
+    gathered = send(mine, ("z", "y"))
+
+    drafted = drafted_key_value.transpose(0, 1, 3, 2, 4).reshape(COUNT, 2, WIDTH)
+    bias, fresh_bias, fresh_keys, fresh_values, held = call(
+        prepare,
+        (
+            shape((ROWS, pages * page_len), f32),
+            shape((ROWS, GROUP * STEPS, COUNT), f32),
+            shape((COUNT, WIDTH), bf16),
+            shape((COUNT, WIDTH), bf16),
+            shape(paged_key_value.shape, bf16),
+        ),
+        "vsssvh",
+        [dma((1,))],
+        limit=8 * 2**20,
+    )(block_table, page_count, tail_fill, seq_index.reshape(1), drafted, paged_key_value)
+    block, weight, gates = call(
+        attend,
+        (
+            shape((SIDE, 40, WIDTH), bf16),
+            shape(out_weight.shape, bf16),
+            shape(gate_up.shape, bf16),
+        ),
+        "vvvvvvhh",
+        [pltpu.VMEM((SIDE, 40, WIDTH), f32), dma((2,))],
+    )(gathered, held, fresh_keys, fresh_values, bias, fresh_bias, out_weight, gate_up)
+    block = call(join, shape((SIDE, 40, WIDTH), bf16), "v")(send(block, "y"))
+    attended = call(finish, shape((SIDE, 32, WIDTH), bf16), "v")(send(block, "z"))
+    partial_sum = call(project, shape((SIDE, COUNT, columns), bf16), "vv")(
+        send(attended, "y"), weight
     )
     scaled, stream = call(
         normalise,
-        (shape((SIDE, 40, WIDTH), bf16), shape((STEPS, ROWS, columns), f32)),
-    )(
-        send(partial_sum, ("x", "core")),
-        stream_in.reshape(COUNT, columns),
-        norm_gain.reshape(1, columns),
-    )
-    scaled = lax.all_gather(send(scaled, "y"), "z").reshape(seq_count, 40, WIDTH)
-    hidden = call(feed, shape((STEPS, ROWS, units), bf16))(scaled, gate_up)
+        (shape((seq_count, 40, WIDTH), bf16), shape((STEPS, ROWS, columns), f32)),
+        "vvv",
+        [pltpu.VMEM((COUNT, columns), f32)],
+    )(send(partial_sum, ("x", "core")), stream_in, norm_gain.reshape(1, columns))
+    hidden = call(feed, shape((STEPS, ROWS, units), bf16), "vv")(
+        send(scaled, ("z", "y")), gates
+    )
     return hidden, stream
 
 

time: 123 us -> 110 us (0.89)
  blocking collectives: 58.5 us -> 71.6 us
  waiting for transfers between devices: 14 us -> 4.89 us
  starting transfers between devices: 25.6 us -> 16.6 us
  local copies, waits for them, and re-layouts: 13.7 us -> 8.56 us
  other arithmetic: 3.21 us -> 0 us
    all_to_all x3 -> x5, blocking collectives: 32.8 us -> 71.6 us  [send(): return lax.all_to_all(x, axis, split_axis=0, concat_axis=0, tiled=True)]
    all_gather x1 -> x0, blocking collectives: 25.7 us -> none  [shards(): lax.all_gather(send(scaled, 'y'), 'z').reshape(seq_count, 40, WIDTH)]
    all_to_all x3 -> x1, waiting for transfers between devices: 14 us -> 4.89 us  [send(): return lax.all_to_all(x, axis, split_axis=0, concat_axis=0, tiled=True)]
    all_to_all x3 -> x1, starting transfers between devices: 25.6 us -> 16.6 us  [send(): return lax.all_to_all(x, axis, split_axis=0, concat_axis=0, tiled=True)]
    unnamed x12 -> x21, local copies, waits for them, and re-layouts: 10.7 us -> 8.56 us
    broadcast_in_dim x2 -> x0, local copies, waits for them, and re-layouts: 1.41 us -> none  [shards(): jnp.broadcast_to(mine[None], (seq_count, *mine.shape))]
    pallas_call x6 -> x8, Pallas kernels: 6.34 us -> 7.33 us  [the longest x1 2.69 us: shards(): call(attend, (shape((SIDE, 40, WIDTH), bf16), shape(out_weight.shape, bf1...]
  transfers between devices with their start and end apart: 3 -> 1, of which waited for: 3 -> 1; matrix products, arithmetic and copies ran while one was open for 9% -> 5% of each run, Pallas kernels for 0% -> 1%
where the time goes in v3:
time: 110 us
  blocking collectives  71.6 us (65%)
  starting transfers between devices  16.6 us (15%)
  local copies, waits for them, and re-layouts  8.56 us (8%)
  Pallas kernels  7.33 us (7%)
  waiting for transfers between devices  4.89 us (4%)
    all_to_all x5, blocking collectives, send(): return lax.all_to_all(x, axis, split_axis=0, concat_axis=0, tiled=True)  71.6 us
    all_to_all x1, starting transfers between devices, send(): return lax.all_to_all(x, axis, split_axis=0, concat_axis=0, tiled=True)  16.6 us
    unnamed x21, local copies, waits for them, and re-layouts  8.56 us
    all_to_all x1, waiting for transfers between devices, send(): return lax.all_to_all(x, axis, split_axis=0, concat_axis=0, tiled=True)  4.89 us
    pallas_call x1, Pallas kernels, shards(): call(attend, (shape((SIDE, 40, WIDTH), bf16), shape(out_weight.shape, bf1...  2.69 us
  transfers between devices with their start and end apart: 1, of which 1 were waited for; matrix products, arithmetic and copies ran while one was open for 5% of the time, Pallas kernels for 1%

profile of v3, /device:TPU:8, one launch (start us, length us, event | category | flops | bytes accessed | tf_op | source)
XLA Modules:
  0.0 109.7 jit_solution(3822677126434895180)
XLA Ops:
  0.6 0.0 copy-start.2
  0.6 0.0 copy-start.4
  0.7 0.0 copy-start.5
  0.7 0.7 copy-done.5
  1.4 0.0 copy-start.6
  1.4 0.0 copy-start.8
  1.4 0.7 shard_map.113
  2.1 16.6 %all-to-all-start = ((bf16[64,4,128]{2,1,0:T(4,128)(2,1)}), bf16[64,4,128]{2,1,0:T(4,128)(2,1)S(1)}, u32[]{:S(2)}, u32[]{:S(2)}) async-start(bf16[64,4,128]{2,1,0:T(4,128)(2,1)} %shard_map.113), calls=%async_computation | async-start | bytes 131072 | tf_op jit(solution)/shard_map/all_to_all | solution.py:244
  18.7 0.0 copy-start.1
  18.7 5.8 %copy.12.gate_up = bf16[2,52,16384]{2,1,0:T(8,128)(2,1)} copy(bf16[2,52,16384]{2,0,1:T(2,128)(2,1)} %param.19) | data formatting | bytes 6815744 | tf_op args[9]
  24.5 0.0 copy-done.2
  24.5 0.0 copy-done.4
  24.5 0.0 copy-done.6
  24.5 0.0 copy-done.8
  24.5 0.0 copy-done.9
  24.5 0.7 shard_map.114
  25.2 4.9 %all-to-all-done.gathered = bf16[64,4,128]{2,1,0:T(4,128)(2,1)S(1)} async-done(((bf16[64,4,128]{2,1,0:T(4,128)(2,1)}), bf16[64,4,128]{2,1,0:T(4,128)(2,1)S(1)}, u32[]{:S(2)}, u32[]{:S(2)}) %all-to-all-start) | async-done | bytes 65568 | tf_op jit(solution)/shard_map/all_to_all | solution.py:244
  30.1 0.0 copy-done.1
  30.1 2.0 %copy-done = bf16[2,52,16384]{2,1,0:T(8,128)(2,1)S(1)} copy-done((bf16[2,52,16384]{2,1,0:T(8,128)(2,1)S(1)}, bf16[2,52,16384]{2,1,0:T(8,128)(2,1)}, u32[]{:S(2)}) %copy-start) | copy-done | bytes 3407896
  32.1 2.7 %shard_map.115 = (bf16[8,40,128]{2,1,0:T(8,128)(2,1)S(1)}, bf16[2048,256]{1,0:T(8,128)(2,1)S(1)}, bf16[2,52,16384]{2,1,0:T(8,128)(2,1)S(1)}) custom-call(bf16[64,4,128]{2,1,0:T(4,128)(2,1)S(1)} %all-to-all-done.gathered, bf16[2,1,8,128,128]{4,3,2,1,0:T(8,128)(2,1)S(1)} %get-tuple-element.12.paged, bf16[16,128]{1,0:T(8,128)(2,1)S(1)} %get-tuple-element.13.fresh_keys, ...), custom_call_target="tpu_custom_call" | custom-call | tf_op jit(solution)/shard_map/pallas_call | solution.py:284
  34.8 10.8 %all_to_all.30.got = bf16[8,40,128]{2,1,0:T(8,128)(2,1)S(1)} all-to-all(bf16[8,40,128]{2,1,0:T(8,128)(2,1)S(1)} %get-tuple-element.17), channel_id=1, replica_groups=mesh['x'=4,'core'=2,'z'=8,'y'=8] {'y'}, dimensions={0} | all-to-all | bytes 163840 | tf_op jit(solution)/shard_map/all_to_all | solution.py:244
  45.6 0.2 shard_map.116
  45.8 13.6 %all_to_all.31.got = bf16[8,40,128]{2,1,0:T(8,128)(2,1)S(1)} all-to-all(bf16[8,40,128]{2,1,0:T(8,128)(2,1)S(1)} %shard_map.116), channel_id=1, replica_groups=mesh['x'=4,'core'=2,'z'=8,'y'=8] {'z'}, dimensions={0} | all-to-all | bytes 163840 | tf_op jit(solution)/shard_map/all_to_all | solution.py:244
  59.4 0.3 shard_map.117
  59.7 10.8 %all_to_all.32.attended = bf16[8,32,128]{2,1,0:T(8,128)(2,1)S(1)} all-to-all(bf16[8,32,128]{2,1,0:T(8,128)(2,1)S(1)} %shard_map.117), channel_id=1, replica_groups=mesh['x'=4,'core'=2,'z'=8,'y'=8] {'y'}, dimensions={0} | all-to-all | bytes 131072 | tf_op jit(solution)/shard_map/all_to_all | solution.py:244
  70.5 0.2 shard_map.118
  70.8 9.7 %all_to_all.33.parts = bf16[8,16,256]{2,1,0:T(8,128)(2,1)S(1)} all-to-all(bf16[8,16,256]{2,1,0:T(8,128)(2,1)S(1)} %shard_map.118), channel_id=1, replica_groups=mesh['x'=4,'core'=2,'z'=8,'y'=8] {'x','core'}, dimensions={0} | all-to-all | bytes 131072 | tf_op jit(solution)/shard_map/all_to_all | solution.py:244
  80.5 0.0 copy-done.3
  80.5 0.0 copy-done.7
  80.5 0.6 shard_map.119
  81.1 26.8 %all_to_all.34.got = bf16[64,40,128]{2,1,0:T(8,128)(2,1)S(1)} all-to-all(bf16[64,40,128]{2,1,0:T(8,128)(2,1)S(1)} %get-tuple-element.19), channel_id=1, replica_groups=mesh['x'=4,'core'=2,'z'=8,'y'=8] {'z','y'}, dimensions={0} | all-to-all | bytes 1310720 | tf_op jit(solution)/shard_map/all_to_all | solution.py:244
  107.9 1.8 %shard_map.120 = bf16[4,4,52]{2,1,0:T(4,128)(2,1)} custom-call(bf16[64,40,128]{2,1,0:T(8,128)(2,1)S(1)} %all_to_all.34.got, bf16[2,52,16384]{2,1,0:T(8,128)(2,1)S(1)} %get-tuple-element.20.weight), custom_call_target="tpu_custom_call" | custom-call | tf_op jit(solution)/shard_map/pallas_call | solution.py:305
  (4 shorter events, 0.0 us)
Async XLA Ops:
  0.6 23.9 %copy-start.2 = (bf16[2,1,8,128,128]{4,3,2,1,0:T(8,128)(2,1)S(1)}, bf16[2,1,8,128,128]{4,3,2,1,0:T(8,128)(2,1)}, u32[]{:S(2)}) copy-start(bf16[2,1,8,128,128]{4,3,2,1,0:T(8,128)(2,1)} %paged.1) | copy-start | bytes 1572868
  0.6 23.8 %copy-start.4 = (bf16[4,4,2,1,128]{4,2,3,1,0:T(2,128)(2,1)S(1)}, bf16[4,4,2,1,128]{4,2,3,1,0:T(2,128)(2,1)}, u32[]{:S(2)}) copy-start(bf16[4,4,2,1,128]{4,2,3,1,0:T(2,128)(2,1)} %param.11) | copy-start | bytes 24580
  0.7 0.7 copy-start.5
  1.4 23.1 %copy-start.6 = (s32[4,128]{1,0:T(4,128)S(1)}, s32[4,128]{1,0:T(4,128)}, u32[]{:S(2)}) copy-start(s32[4,128]{1,0:T(4,128)} %table.1) | copy-start | bytes 6148
  1.4 23.1 %copy-start.8 = (s32[4]{0:T(128)S(1)}, s32[4]{0:T(128)}, u32[]{:S(2)}) copy-start(s32[4]{0:T(128)} %count.1) | copy-start | bytes 52
  1.4 23.1 %copy-start.9 = (s32[4]{0:T(128)S(1)}, s32[4]{0:T(128)}, u32[]{:S(2)}) copy-start(s32[4]{0:T(128)} %tail.1) | copy-start | bytes 52
  2.1 28.0 %all-to-all-start = ((bf16[64,4,128]{2,1,0:T(4,128)(2,1)}), bf16[64,4,128]{2,1,0:T(4,128)(2,1)S(1)}, u32[]{:S(2)}, u32[]{:S(2)}) async-start(bf16[64,4,128]{2,1,0:T(4,128)(2,1)} %shard_map.113), calls=%async_computation | async-start | bytes 131072 | tf_op jit(solution)/shard_map/all_to_all | solution.py:244
  18.7 11.4 %copy-start.1 = (bf16[2048,256]{1,0:T(8,128)(2,1)S(1)}, bf16[2048,256]{1,0:T(8,128)(2,1)}, u32[]{:S(2)}) copy-start(bf16[2048,256]{1,0:T(8,128)(2,1)} %out_weight.1) | copy-start | bytes 3145732
  30.1 2.0 %copy-start = (bf16[2,52,16384]{2,1,0:T(8,128)(2,1)S(1)}, bf16[2,52,16384]{2,1,0:T(8,128)(2,1)}, u32[]{:S(2)}) copy-start(bf16[2,52,16384]{2,1,0:T(8,128)(2,1)} %copy.12.gate_up) | copy-start | bytes 10223620
  32.1 48.3 %copy-start.3 = (f32[4,4,256]{2,1,0:T(4,128)S(1)}, f32[4,4,256]{2,1,0:T(4,128)}, u32[]{:S(2)}) copy-start(f32[4,4,256]{2,1,0:T(4,128)} %stream_in.1) | copy-start | bytes 49156
  32.1 48.3 %copy-start.7 = (f32[256]{0:T(256)S(1)}, f32[256]{0:T(256)}, u32[]{:S(2)}) copy-start(f32[256]{0:T(256)} %param.18) | copy-start | bytes 3076

commit v4 on v3

--- a/solution.py
+++ b/solution.py
@@ -40,13 +40,14 @@
     return hi, x - hi
 
 
-def call(body, out_shape, inputs="", scratch=(), limit=32 * 2**20):
+def call(body, out_shape, inputs="", scratch=(), limit=32 * 2**20, moved=2**24):
     spaces = {"v": pltpu.VMEM, "h": pl.ANY, "s": pltpu.SMEM}
     return pl.pallas_call(
         body,
         out_shape=out_shape,
         in_specs=[pl.BlockSpec(memory_space=spaces[c]) for c in inputs],
         scratch_shapes=list(scratch),
+        cost_estimate=pl.CostEstimate(flops=2**26, bytes_accessed=moved, transcendentals=2**18),
         compiler_params=pltpu.CompilerParams(vmem_limit_bytes=limit),
     )
 
@@ -62,6 +63,10 @@
     x = queries[...].astype(f32)
     x = jnp.concatenate([x[:, r, :] for r in range(ROWS)], axis=1).astype(bf16)
     out[...] = jnp.broadcast_to(x[None], out.shape)
+
+
+def tie(table, weight, out):
+    out[...] = table[...]
 
 
 def prepare(
@@ -101,15 +106,9 @@
     fresh_values,
     bias,
     fresh_bias,
-    out_weight,
-    gate_up,
     out,
-    out_weight_held,
-    gate_up_held,
     block,
-    sems,
 ):
-    moves = begin([(out_weight, out_weight_held), (gate_up, gate_up_held)], sems)
     sent = jnp.concatenate([gathered[:, i, :].astype(f32) for i in range(STEPS)], axis=0)
     shape = (STEPS * GROUP * 4, WIDTH)
     quarter = iota(shape, 0) % 4
@@ -158,8 +157,6 @@
         jnp.sum(stats, axis=1, keepdims=True), (SIDE, 8, WIDTH)
     )
     out[...] = block[...].astype(bf16)
-    for move in moves:
-        move.wait()
 
 
 def merged(got):
@@ -268,6 +265,9 @@
     gathered = send(mine, ("z", "y"))
 
     drafted = drafted_key_value.transpose(0, 1, 3, 2, 4).reshape(COUNT, 2, WIDTH)
+    table = call(tie, shape(block_table.shape, jnp.int32), "vh", limit=62 * 2**20)(
+        block_table, gate_up
+    )
     bias, fresh_bias, fresh_keys, fresh_values, held = call(
         prepare,
         (
@@ -280,21 +280,17 @@
         "vsssvh",
         [dma((1,))],
         limit=8 * 2**20,
-    )(block_table, page_count, tail_fill, seq_index.reshape(1), drafted, paged_key_value)
-    block, weight, gates = call(
+    )(table, page_count, tail_fill, seq_index.reshape(1), drafted, paged_key_value)
+    block = call(
         attend,
-        (
-            shape((SIDE, 40, WIDTH), bf16),
-            shape(out_weight.shape, bf16),
-            shape(gate_up.shape, bf16),
-        ),
-        "vvvvvvhh",
-        [pltpu.VMEM((SIDE, 40, WIDTH), f32), dma((2,))],
-    )(gathered, held, fresh_keys, fresh_values, bias, fresh_bias, out_weight, gate_up)
+        shape((SIDE, 40, WIDTH), bf16),
+        "vvvvvv",
+        [pltpu.VMEM((SIDE, 40, WIDTH), f32)],
+    )(gathered, held, fresh_keys, fresh_values, bias, fresh_bias)
     block = call(join, shape((SIDE, 40, WIDTH), bf16), "v")(send(block, "y"))
     attended = call(finish, shape((SIDE, 32, WIDTH), bf16), "v")(send(block, "z"))
     partial_sum = call(project, shape((SIDE, COUNT, columns), bf16), "vv")(
-        send(attended, "y"), weight
+        send(attended, "y"), out_weight
     )
     scaled, stream = call(
         normalise,
@@ -303,7 +299,7 @@
         [pltpu.VMEM((COUNT, columns), f32)],
     )(send(partial_sum, ("x", "core")), stream_in, norm_gain.reshape(1, columns))
     hidden = call(feed, shape((STEPS, ROWS, units), bf16), "vv")(
-        send(scaled, ("z", "y")), gates
+        send(scaled, ("z", "y")), gate_up
     )
     return hidden, stream
 

time: 110 us -> 110 us (level)
  waiting for transfers between devices: 4.89 us -> 2.87 us
  blocking collectives: 71.6 us -> 73.6 us
  local copies, waits for them, and re-layouts: 8.56 us -> 7.12 us
    all_to_all x5, blocking collectives: 71.6 us -> 73.6 us  [send(): return lax.all_to_all(x, axis, split_axis=0, concat_axis=0, tiled=True)]
    all_to_all x1, waiting for transfers between devices: 4.89 us -> 2.87 us  [send(): return lax.all_to_all(x, axis, split_axis=0, concat_axis=0, tiled=True)]
    unnamed x21, local copies, waits for them, and re-layouts: 8.56 us -> 7.12 us
    pallas_call x1 -> x2, Pallas kernels: 2.69 us -> 3.69 us  [the longest x1 2.34 us: shards(): call(attend, shape((SIDE, 40, WIDTH), bf16), 'vvvvvv', [pltpu.VMEM((SIDE,...]
  transfers between devices with their start and end apart: 1 -> 1, of which waited for: 1 -> 1; matrix products, arithmetic and copies ran while one was open for 5% -> 5% of each run, Pallas kernels for 1% -> 2%
where the time goes in v4:
time: 110 us; the launch traced here: 109 us
  blocking collectives  73.6 us (67%)
  starting transfers between devices  16.6 us (15%)
  Pallas kernels  8.33 us (8%)
  local copies, waits for them, and re-layouts  7.12 us (6%)
  waiting for transfers between devices  2.87 us (3%)
    all_to_all x5, blocking collectives, send(): return lax.all_to_all(x, axis, split_axis=0, concat_axis=0, tiled=True)  73.6 us
    all_to_all x1, starting transfers between devices, send(): return lax.all_to_all(x, axis, split_axis=0, concat_axis=0, tiled=True)  16.6 us
    unnamed x21, local copies, waits for them, and re-layouts  7.12 us
    all_to_all x1, waiting for transfers between devices, send(): return lax.all_to_all(x, axis, split_axis=0, concat_axis=0, tiled=True)  2.87 us
    pallas_call x1, Pallas kernels, shards(): call(attend, shape((SIDE, 40, WIDTH), bf16), 'vvvvvv', [pltpu.VMEM((SIDE,...  2.34 us
  transfers between devices with their start and end apart: 1, of which 1 were waited for; matrix products, arithmetic and copies ran while one was open for 5% of the time, Pallas kernels for 2%

profile of v4, /device:TPU:8, one launch (start us, length us, event | category | flops | bytes accessed | tf_op | source)
XLA Modules:
  0.0 109.3 jit_solution(17002002563520928105)
XLA Ops:
  0.6 0.0 copy-start.8
  0.6 0.7 copy-done.8
  1.3 0.7 shard_map.113
  2.0 16.6 %all-to-all-start = ((bf16[64,4,128]{2,1,0:T(4,128)(2,1)}), bf16[64,4,128]{2,1,0:T(4,128)(2,1)S(1)}, u32[]{:S(2)}, u32[]{:S(2)}) async-start(bf16[64,4,128]{2,1,0:T(4,128)(2,1)} %shard_map.113), calls=%async_computation | async-start | bytes 131072 | tf_op jit(solution)/shard_map/all_to_all | solution.py:241
  18.6 0.0 copy-start.2
  18.6 0.0 copy-start.3
  18.7 0.0 copy-start.5
  18.7 0.0 copy-start.6
  18.7 5.7 %copy.12.weight = bf16[2,52,16384]{2,1,0:T(8,128)(2,1)} copy(bf16[2,52,16384]{2,0,1:T(2,128)(2,1)} %param.19) | data formatting | bytes 6815744 | tf_op args[9]
  24.4 1.3 %shard_map.114.table = s32[4,128]{1,0:T(4,128)} custom-call(s32[4,128]{1,0:T(4,128)} %table.1, bf16[2,52,16384]{2,1,0:T(8,128)(2,1)} %copy.12.weight), custom_call_target="tpu_custom_call" | custom-call | flops 67108864 | bytes 16777216 | tf_op jit(solution)/shard_map/pallas_call | solution.py:268
  25.8 0.0 copy-done.2
  25.8 0.0 copy-done.3
  25.8 0.0 copy-done.5
  25.8 0.0 copy-done.6
  25.8 0.0 copy-start.4
  25.8 0.7 copy-done.4
  26.5 0.7 shard_map.115
  27.2 2.9 %all-to-all-done.gathered = bf16[64,4,128]{2,1,0:T(4,128)(2,1)S(1)} async-done(((bf16[64,4,128]{2,1,0:T(4,128)(2,1)}), bf16[64,4,128]{2,1,0:T(4,128)(2,1)S(1)}, u32[]{:S(2)}, u32[]{:S(2)}) %all-to-all-start) | async-done | bytes 65568 | tf_op jit(solution)/shard_map/all_to_all | solution.py:241
  30.0 2.3 %shard_map.116 = bf16[8,40,128]{2,1,0:T(8,128)(2,1)S(1)} custom-call(bf16[64,4,128]{2,1,0:T(4,128)(2,1)S(1)} %all-to-all-done.gathered, bf16[2,1,8,128,128]{4,3,2,1,0:T(8,128)(2,1)S(1)} %get-tuple-element.9.paged, bf16[16,128]{1,0:T(8,128)(2,1)S(1)} %get-tuple-element.10.fresh_keys, bf16[16,128]{1,0:T(8,128)(2,1)S(1)} %get-tuple-element.11.fresh_values, ...), custom_call_target="tpu_custom_call" | custom-call | flops 67108864 | bytes 16777216 | tf_op jit(solution)/shard_map/pallas_call | solution.py:284
  32.4 11.3 %all_to_all.30.got = bf16[8,40,128]{2,1,0:T(8,128)(2,1)S(1)} all-to-all(bf16[8,40,128]{2,1,0:T(8,128)(2,1)S(1)} %shard_map.116), channel_id=1, replica_groups=mesh['x'=4,'core'=2,'z'=8,'y'=8] {'y'}, dimensions={0} | all-to-all | bytes 163840 | tf_op jit(solution)/shard_map/all_to_all | solution.py:241
  43.6 0.2 shard_map.117
  43.9 15.1 %all_to_all.31.got = bf16[8,40,128]{2,1,0:T(8,128)(2,1)S(1)} all-to-all(bf16[8,40,128]{2,1,0:T(8,128)(2,1)S(1)} %shard_map.117), channel_id=1, replica_groups=mesh['x'=4,'core'=2,'z'=8,'y'=8] {'z'}, dimensions={0} | all-to-all | bytes 163840 | tf_op jit(solution)/shard_map/all_to_all | solution.py:241
  59.0 0.3 shard_map.118
  59.3 10.8 %all_to_all.32.attended = bf16[8,32,128]{2,1,0:T(8,128)(2,1)S(1)} all-to-all(bf16[8,32,128]{2,1,0:T(8,128)(2,1)S(1)} %shard_map.118), channel_id=1, replica_groups=mesh['x'=4,'core'=2,'z'=8,'y'=8] {'y'}, dimensions={0} | all-to-all | bytes 131072 | tf_op jit(solution)/shard_map/all_to_all | solution.py:241
  70.1 0.0 copy-done.1
  70.1 0.3 shard_map.119
  70.3 9.7 %all_to_all.33.parts = bf16[8,16,256]{2,1,0:T(8,128)(2,1)S(1)} all-to-all(bf16[8,16,256]{2,1,0:T(8,128)(2,1)S(1)} %shard_map.119), channel_id=1, replica_groups=mesh['x'=4,'core'=2,'z'=8,'y'=8] {'x','core'}, dimensions={0} | all-to-all | bytes 131072 | tf_op jit(solution)/shard_map/all_to_all | solution.py:241
  80.0 0.0 copy-done.7
  80.0 0.0 copy-done.9
  80.0 0.6 shard_map.120
  80.7 26.8 %all_to_all.34.got = bf16[64,40,128]{2,1,0:T(8,128)(2,1)S(1)} all-to-all(bf16[64,40,128]{2,1,0:T(8,128)(2,1)S(1)} %get-tuple-element.14), channel_id=1, replica_groups=mesh['x'=4,'core'=2,'z'=8,'y'=8] {'z','y'}, dimensions={0} | all-to-all | bytes 1310720 | tf_op jit(solution)/shard_map/all_to_all | solution.py:241
  107.4 1.8 %shard_map.121 = bf16[4,4,52]{2,1,0:T(4,128)(2,1)} custom-call(bf16[64,40,128]{2,1,0:T(8,128)(2,1)S(1)} %all_to_all.34.got, bf16[2,52,16384]{2,1,0:T(8,128)(2,1)S(1)} %copy-done), custom_call_target="tpu_custom_call" | custom-call | flops 67108864 | bytes 16777216 | tf_op jit(solution)/shard_map/pallas_call | solution.py:301
  (5 shorter events, 0.0 us)
Async XLA Ops:
  0.6 0.7 copy-start.8
  2.0 28.0 %all-to-all-start = ((bf16[64,4,128]{2,1,0:T(4,128)(2,1)}), bf16[64,4,128]{2,1,0:T(4,128)(2,1)S(1)}, u32[]{:S(2)}, u32[]{:S(2)}) async-start(bf16[64,4,128]{2,1,0:T(4,128)(2,1)} %shard_map.113), calls=%async_computation | async-start | bytes 131072 | tf_op jit(solution)/shard_map/all_to_all | solution.py:241
  18.6 7.1 %copy-start.2 = (bf16[2,1,8,128,128]{4,3,2,1,0:T(8,128)(2,1)S(1)}, bf16[2,1,8,128,128]{4,3,2,1,0:T(8,128)(2,1)}, u32[]{:S(2)}) copy-start(bf16[2,1,8,128,128]{4,3,2,1,0:T(8,128)(2,1)} %paged.1) | copy-start | bytes 1572868
  18.6 7.1 %copy-start.3 = (bf16[4,4,2,1,128]{4,2,3,1,0:T(2,128)(2,1)S(1)}, bf16[4,4,2,1,128]{4,2,3,1,0:T(2,128)(2,1)}, u32[]{:S(2)}) copy-start(bf16[4,4,2,1,128]{4,2,3,1,0:T(2,128)(2,1)} %param.11) | copy-start | bytes 24580
  18.7 7.1 %copy-start.5 = (s32[4]{0:T(128)S(1)}, s32[4]{0:T(128)}, u32[]{:S(2)}) copy-start(s32[4]{0:T(128)} %count.1) | copy-start | bytes 52
  18.7 7.1 %copy-start.6 = (s32[4]{0:T(128)S(1)}, s32[4]{0:T(128)}, u32[]{:S(2)}) copy-start(s32[4]{0:T(128)} %tail.1) | copy-start | bytes 52
  24.4 45.7 %copy-start.1 = (bf16[2048,256]{1,0:T(8,128)(2,1)S(1)}, bf16[2048,256]{1,0:T(8,128)(2,1)}, u32[]{:S(2)}) copy-start(bf16[2048,256]{1,0:T(8,128)(2,1)} %weight.3) | copy-start | bytes 3145732
  24.4 55.6 %copy-start.7 = (f32[4,4,256]{2,1,0:T(4,128)S(1)}, f32[4,4,256]{2,1,0:T(4,128)}, u32[]{:S(2)}) copy-start(f32[4,4,256]{2,1,0:T(4,128)} %stream_in.1) | copy-start | bytes 49156
  24.4 55.6 %copy-start.9 = (f32[256]{0:T(256)S(1)}, f32[256]{0:T(256)}, u32[]{:S(2)}) copy-start(f32[256]{0:T(256)} %param.18) | copy-start | bytes 3076
  25.8 0.7 copy-start.4
  30.0 77.4 %copy-start = (bf16[2,52,16384]{2,1,0:T(8,128)(2,1)S(1)}, bf16[2,52,16384]{2,1,0:T(8,128)(2,1)}, u32[]{:S(2)}) copy-start(bf16[2,52,16384]{2,1,0:T(8,128)(2,1)} %copy.12.weight) | copy-start | bytes 10223620

commit v5 on v4

--- a/solution.py
+++ b/solution.py
@@ -120,84 +120,67 @@
         pick_row % STEPS == pick_col // (4 * GROUP)
     )
     pick = jnp.where(pick, 1.0, 0.0).astype(bf16)
-    keys = paged[0, 0].reshape(-1, WIDTH)
-    values = paged[1, 0].reshape(-1, WIDTH)
-    fresh_k = fresh_keys[...]
-    fresh_v = fresh_values[...]
-    ones = jnp.ones((keys.shape[0], WIDTH), bf16)
-    fresh_ones = jnp.ones((fresh_k.shape[0], WIDTH), bf16)
-    scale = WIDTH ** (-0.5)
-    lane = iota((GROUP * STEPS, WIDTH), 1)
-    place = iota((GROUP * STEPS, WIDTH), 0) % 8
-    stats = None
+    placed = []
     for r in range(ROWS):
         chosen = turned[(3 - r) % 4]
         for c in range(3):
             chosen = jnp.where(quarter == c, turned[(c - r) % 4], chosen)
-        chosen = jnp.where(diagonal, chosen, 0.0).astype(bf16)
-        query = dot(pick, chosen).astype(bf16)
-        scores = dot_t(query, keys) * scale + bias[r : r + 1, :]
-        fresh = dot_t(query, fresh_k) * scale + fresh_bias[r]
-        peak = jnp.maximum(
-            jnp.max(scores, axis=1, keepdims=True), jnp.max(fresh, axis=1, keepdims=True)
-        )
-        peak = jnp.maximum(peak, floor).astype(bf16).astype(f32)
-        weights = jnp.exp(scores - peak).astype(bf16)
-        fresh_weights = jnp.exp(fresh - peak).astype(bf16)
-        total = dot(weights, ones) + dot(fresh_weights, fresh_ones)
-        summed = dot(weights, values) + dot(fresh_weights, fresh_v)
-        mean = summed / jnp.where(total > 0.0, total, 1.0)
-        block[:, 8 * r : 8 * r + 8, :] = mean.reshape(SIDE, 8, WIDTH)
-        hi, rest = split(total)
-        at = lane - place - 8 * r
-        stat = jnp.where(at == 0, peak, jnp.where(at == 32, hi, jnp.where(at == 64, rest, 0.0)))
-        stats = stat if stats is None else stats + stat
-    stats = stats.reshape(SIDE, 8, WIDTH)
-    block[:, 32:40, :] = jnp.broadcast_to(
-        jnp.sum(stats, axis=1, keepdims=True), (SIDE, 8, WIDTH)
-    )
+        placed.append(jnp.where(diagonal, chosen, 0.0).astype(bf16))
+    query = dot(pick, jnp.concatenate(placed, axis=1)).astype(bf16)
+    query = jnp.concatenate([query[:, r * WIDTH : (r + 1) * WIDTH] for r in range(ROWS)], axis=0)
+    keys = paged[0, 0].reshape(-1, WIDTH)
+    values = paged[1, 0].reshape(-1, WIDTH)
+    values = jnp.concatenate([values, jnp.ones(values.shape, bf16)], axis=1)
+    fresh_v = fresh_values[...]
+    fresh_v = jnp.concatenate([fresh_v, jnp.ones(fresh_v.shape, bf16)], axis=1)
+    each = GROUP * STEPS
+    masks = [jnp.broadcast_to(bias[r : r + 1, :], (each, bias.shape[1])) for r in range(ROWS)]
+    fresh_masks = [fresh_bias[r] for r in range(ROWS)]
+    scale = WIDTH ** (-0.5)
+    scores = dot_t(query, keys) * scale + jnp.concatenate(masks, axis=0)
+    fresh = dot_t(query, fresh_keys[...]) * scale + jnp.concatenate(fresh_masks, axis=0)
+    peak = jnp.maximum(
+        jnp.max(scores, axis=1, keepdims=True), jnp.max(fresh, axis=1, keepdims=True)
+    )
+    peak = jnp.maximum(peak, floor).astype(bf16).astype(f32)
+    weights = jnp.exp(scores - peak).astype(bf16)
+    fresh_weights = jnp.exp(fresh - peak).astype(bf16)
+    summed = dot(weights, values) + dot(fresh_weights, fresh_v)
+    total = summed[:, WIDTH:]
+    mean = summed[:, :WIDTH] / jnp.where(total > 0.0, total, 1.0)
+    hi, rest = split(total)
+    lane = iota(total.shape, 1)
+    stat = jnp.where(lane == 0, peak, jnp.where(lane == 1, hi, rest))
+    for r in range(ROWS):
+        block[:, r, :] = mean[r * each : (r + 1) * each]
+        block[:, ROWS + r, :] = stat[r * each : (r + 1) * each]
     out[...] = block[...].astype(bf16)
 
 
-def merged(got):
+def finish(got, out):
+    n = got.shape[0]
     parts = got[...].astype(f32)
-    n = parts.shape[0]
-    means, stats = parts[:, :32, :], parts[:, 32:40, :]
-    stats = jnp.concatenate([stats] * 4, axis=1).reshape(n * 32, WIDTH)
-    at = iota((n * 32, WIDTH), 1) - iota((n * 32, WIDTH), 0) % 32
+    flat = parts.reshape(n * 8, WIDTH)
+    lane = iota(flat.shape, 1)
     ones = jnp.ones((WIDTH, WIDTH), bf16)
-    peaks = dot(jnp.where(at == 0, stats, 0.0).astype(bf16), ones).reshape(n, 32, WIDTH)
-    totals = dot(jnp.where((at == 32) | (at == 64), stats, 0.0).astype(bf16), ones)
-    totals = totals.reshape(n, 32, WIDTH)
-    peak = jnp.max(peaks, axis=0)
-    factors = jnp.exp(peaks - peak[None]) * totals
-    total = jnp.sum(factors, axis=0)
-    mean = jnp.sum(factors * means, axis=0) / jnp.where(total > 0.0, total, 1.0)
-    return peak, total, mean
-
-
-def join(got, out):
-    peak, total, mean = merged(got)
-    hi, rest = split(total)
-    at = iota((32, WIDTH), 1) - iota((32, WIDTH), 0)
-    stat = jnp.where(at == 0, peak, jnp.where(at == 32, hi, jnp.where(at == 64, rest, 0.0)))
-    stat = jnp.broadcast_to(jnp.sum(stat, axis=0, keepdims=True), (8, WIDTH))
-    block = jnp.concatenate([mean, stat], axis=0).astype(bf16)
-    out[...] = jnp.broadcast_to(block[None], out.shape)
-
-
-def finish(got, out):
-    peak, total, mean = merged(got)
-    to, of = iota((32, 32), 0), iota((32, 32), 1)
-    move = (to // 16 == (of // 4) % 2) & ((to // 4) % 4 == of % 4) & (to % 4 == of // 8)
-    moved = dot(jnp.where(move, 1.0, 0.0).astype(bf16), mean.astype(bf16)).astype(bf16)
-    out[...] = jnp.broadcast_to(moved[None], out.shape)
+    peaks = dot(jnp.where(lane == 0, flat, 0.0).astype(bf16), ones).reshape(n, 8, WIDTH)
+    totals = jnp.where((lane == 1) | (lane == 2), flat, 0.0).astype(bf16)
+    totals = dot(totals, ones).reshape(n, 8, WIDTH)
+    factors = jnp.exp(peaks - jnp.max(peaks, axis=0)[None]) * totals
+    factors = pltpu.roll(factors, ROWS, 1)
+    mean = jnp.sum(factors * parts, axis=0) / jnp.sum(factors, axis=0)
+    out[...] = jnp.broadcast_to(mean[:ROWS].astype(bf16)[None], out.shape)
 
 
 def project(attended, weight, out):
+    rows = jnp.concatenate([attended[:, r, :].astype(f32) for r in range(ROWS)], axis=0)
+    shape = (GROUP * COUNT, GROUP * COUNT)
+    to, of = iota(shape, 0), iota(shape, 1)
+    move = (to // COUNT == (of // STEPS) % GROUP) & (to % ROWS == of // (GROUP * STEPS))
+    move = move & ((to // ROWS) % STEPS == of % STEPS)
+    moved = dot(jnp.where(move, 1.0, 0.0).astype(bf16), rows.astype(bf16)).astype(bf16)
     features = jnp.concatenate(
-        [attended[i, COUNT * j : COUNT * (j + 1), :] for i in range(SIDE) for j in range(2)],
-        axis=1,
+        [moved[COUNT * g : COUNT * (g + 1), :] for g in range(GROUP)], axis=1
     )
     out[...] = jnp.broadcast_to(dot(features, weight[...]).astype(bf16)[None], out.shape)
 
@@ -283,14 +266,15 @@
     )(table, page_count, tail_fill, seq_index.reshape(1), drafted, paged_key_value)
     block = call(
         attend,
-        shape((SIDE, 40, WIDTH), bf16),
+        shape((seq_count, 2 * ROWS, WIDTH), bf16),
         "vvvvvv",
-        [pltpu.VMEM((SIDE, 40, WIDTH), f32)],
+        [pltpu.VMEM((seq_count, 2 * ROWS, WIDTH), f32)],
     )(gathered, held, fresh_keys, fresh_values, bias, fresh_bias)
-    block = call(join, shape((SIDE, 40, WIDTH), bf16), "v")(send(block, "y"))
-    attended = call(finish, shape((SIDE, 32, WIDTH), bf16), "v")(send(block, "z"))
+    attended = call(finish, shape((seq_count, ROWS, WIDTH), bf16), "v")(
+        send(block, ("z", "y"))
+    )
     partial_sum = call(project, shape((SIDE, COUNT, columns), bf16), "vv")(
-        send(attended, "y"), out_weight
+        send(attended, ("z", "y")), out_weight
     )
     scaled, stream = call(
         normalise,

time: 110 us -> 109 us (level)
    pallas_call x3 -> x2, Pallas kernels: 2.9 us -> 1.75 us  [the longest x1 1.41 us: shards(): call(attend, shape((seq_count, 2 * ROWS, WIDTH), bf16), 'vvvvvv', [pltpu....]
    all_to_all x5 -> x4, blocking collectives: 73.6 us -> 74 us  [send(): return lax.all_to_all(x, axis, split_axis=0, concat_axis=0, tiled=True)]
where the time goes in v5:
time: 109 us
  blocking collectives  74 us (68%)
  starting transfers between devices  16.6 us (15%)
  Pallas kernels  7.43 us (7%)
  local copies, waits for them, and re-layouts  7.12 us (7%)
  waiting for transfers between devices  2.87 us (3%)
    all_to_all x4, blocking collectives, send(): return lax.all_to_all(x, axis, split_axis=0, concat_axis=0, tiled=True)  74 us
    all_to_all x1, starting transfers between devices, send(): return lax.all_to_all(x, axis, split_axis=0, concat_axis=0, tiled=True)  16.6 us
    unnamed x21, local copies, waits for them, and re-layouts  7.12 us
    all_to_all x1, waiting for transfers between devices, send(): return lax.all_to_all(x, axis, split_axis=0, concat_axis=0, tiled=True)  2.87 us
  transfers between devices with their start and end apart: 1, of which 1 were waited for; matrix products, arithmetic and copies ran while one was open for 5% of the time, Pallas kernels for 2%

profile of v5, /device:TPU:8, one launch (start us, length us, event | category | flops | bytes accessed | tf_op | source)
XLA Modules:
  0.0 108.7 jit_solution(9216770092283662229)
XLA Ops:
  0.6 0.0 copy-start.8
  0.6 0.7 copy-done.8
  1.3 0.7 shard_map.113
  2.0 16.6 %all-to-all-start = ((bf16[64,4,128]{2,1,0:T(4,128)(2,1)}), bf16[64,4,128]{2,1,0:T(4,128)(2,1)S(1)}, u32[]{:S(2)}, u32[]{:S(2)}) async-start(bf16[64,4,128]{2,1,0:T(4,128)(2,1)} %shard_map.113), calls=%async_computation | async-start | bytes 131072 | tf_op jit(solution)/shard_map/all_to_all | solution.py:224
  18.6 0.0 copy-start.2
  18.6 0.0 copy-start.3
  18.7 0.0 copy-start.5
  18.7 0.0 copy-start.6
  18.7 5.7 %copy.12.weight = bf16[2,52,16384]{2,1,0:T(8,128)(2,1)} copy(bf16[2,52,16384]{2,0,1:T(2,128)(2,1)} %param.19) | data formatting | bytes 6815744 | tf_op args[9]
  24.4 0.0 copy-start.1
  24.4 1.3 %shard_map.114.table = s32[4,128]{1,0:T(4,128)} custom-call(s32[4,128]{1,0:T(4,128)} %table.1, bf16[2,52,16384]{2,1,0:T(8,128)(2,1)} %copy.12.weight), custom_call_target="tpu_custom_call" | custom-call | flops 67108864 | bytes 16777216 | tf_op jit(solution)/shard_map/pallas_call | solution.py:251
  25.8 0.0 copy-done.2
  25.8 0.0 copy-done.3
  25.8 0.0 copy-done.5
  25.8 0.0 copy-done.6
  25.8 0.0 copy-start.4
  25.8 0.7 copy-done.4
  26.5 0.7 shard_map.115
  27.2 2.9 %all-to-all-done.gathered = bf16[64,4,128]{2,1,0:T(4,128)(2,1)S(1)} async-done(((bf16[64,4,128]{2,1,0:T(4,128)(2,1)}), bf16[64,4,128]{2,1,0:T(4,128)(2,1)S(1)}, u32[]{:S(2)}, u32[]{:S(2)}) %all-to-all-start) | async-done | bytes 65568 | tf_op jit(solution)/shard_map/all_to_all | solution.py:224
  30.0 1.4 %shard_map.116 = bf16[64,8,128]{2,1,0:T(8,128)(2,1)S(1)} custom-call(bf16[64,4,128]{2,1,0:T(4,128)(2,1)S(1)} %all-to-all-done.gathered, bf16[2,1,8,128,128]{4,3,2,1,0:T(8,128)(2,1)S(1)} %get-tuple-element.9.paged, bf16[16,128]{1,0:T(8,128)(2,1)S(1)} %get-tuple-element.10.fresh_keys, bf16[16,128]{1,0:T(8,128)(2,1)S(1)} %get-tuple-element.11.fresh_values, ...), custom_call_target="tpu_custom_call" | custom-call | flops 67108864 | bytes 16777216 | tf_op jit(solution)/shard_map/pallas_call | solution.py:267
  31.4 21.5 %all_to_all.25.got = bf16[64,8,128]{2,1,0:T(8,128)(2,1)S(1)} all-to-all(bf16[64,8,128]{2,1,0:T(8,128)(2,1)S(1)} %shard_map.116), channel_id=1, replica_groups=mesh['x'=4,'core'=2,'z'=8,'y'=8] {'z','y'}, dimensions={0} | all-to-all | bytes 262144 | tf_op jit(solution)/shard_map/all_to_all | solution.py:224
  53.0 0.3 shard_map.117
  53.3 16.0 %all_to_all.26.attended = bf16[64,4,128]{2,1,0:T(4,128)(2,1)S(1)} all-to-all(bf16[64,4,128]{2,1,0:T(4,128)(2,1)S(1)} %shard_map.117), channel_id=1, replica_groups=mesh['x'=4,'core'=2,'z'=8,'y'=8] {'z','y'}, dimensions={0} | all-to-all | bytes 131072 | tf_op jit(solution)/shard_map/all_to_all | solution.py:224
  69.4 0.0 copy-done.1
  69.4 0.5 shard_map.118
  69.9 9.8 %all_to_all.27.parts = bf16[8,16,256]{2,1,0:T(8,128)(2,1)S(1)} all-to-all(bf16[8,16,256]{2,1,0:T(8,128)(2,1)S(1)} %shard_map.118), channel_id=1, replica_groups=mesh['x'=4,'core'=2,'z'=8,'y'=8] {'x','core'}, dimensions={0} | all-to-all | bytes 131072 | tf_op jit(solution)/shard_map/all_to_all | solution.py:224
  79.6 0.0 copy-done.7
  79.6 0.0 copy-done.9
  79.6 0.6 shard_map.119
  80.2 26.6 %all_to_all.28.got = bf16[64,40,128]{2,1,0:T(8,128)(2,1)S(1)} all-to-all(bf16[64,40,128]{2,1,0:T(8,128)(2,1)S(1)} %get-tuple-element.14), channel_id=1, replica_groups=mesh['x'=4,'core'=2,'z'=8,'y'=8] {'z','y'}, dimensions={0} | all-to-all | bytes 1310720 | tf_op jit(solution)/shard_map/all_to_all | solution.py:224
  106.9 0.0 copy-done
  106.9 1.8 %shard_map.120 = bf16[4,4,52]{2,1,0:T(4,128)(2,1)} custom-call(bf16[64,40,128]{2,1,0:T(8,128)(2,1)S(1)} %all_to_all.28.got, bf16[2,52,16384]{2,1,0:T(8,128)(2,1)S(1)} %copy-done), custom_call_target="tpu_custom_call" | custom-call | flops 67108864 | bytes 16777216 | tf_op jit(solution)/shard_map/pallas_call | solution.py:285
  (3 shorter events, 0.0 us)
Async XLA Ops:
  0.6 0.7 copy-start.8
  2.0 28.0 %all-to-all-start = ((bf16[64,4,128]{2,1,0:T(4,128)(2,1)}), bf16[64,4,128]{2,1,0:T(4,128)(2,1)S(1)}, u32[]{:S(2)}, u32[]{:S(2)}) async-start(bf16[64,4,128]{2,1,0:T(4,128)(2,1)} %shard_map.113), calls=%async_computation | async-start | bytes 131072 | tf_op jit(solution)/shard_map/all_to_all | solution.py:224
  18.6 7.1 %copy-start.2 = (bf16[2,1,8,128,128]{4,3,2,1,0:T(8,128)(2,1)S(1)}, bf16[2,1,8,128,128]{4,3,2,1,0:T(8,128)(2,1)}, u32[]{:S(2)}) copy-start(bf16[2,1,8,128,128]{4,3,2,1,0:T(8,128)(2,1)} %paged.1) | copy-start | bytes 1572868
  18.6 7.1 %copy-start.3 = (bf16[4,4,2,1,128]{4,2,3,1,0:T(2,128)(2,1)S(1)}, bf16[4,4,2,1,128]{4,2,3,1,0:T(2,128)(2,1)}, u32[]{:S(2)}) copy-start(bf16[4,4,2,1,128]{4,2,3,1,0:T(2,128)(2,1)} %param.11) | copy-start | bytes 24580
  18.7 7.1 %copy-start.5 = (s32[4]{0:T(128)S(1)}, s32[4]{0:T(128)}, u32[]{:S(2)}) copy-start(s32[4]{0:T(128)} %count.1) | copy-start | bytes 52
  18.7 7.1 %copy-start.6 = (s32[4]{0:T(128)S(1)}, s32[4]{0:T(128)}, u32[]{:S(2)}) copy-start(s32[4]{0:T(128)} %tail.1) | copy-start | bytes 52
  24.4 45.0 %copy-start.1 = (bf16[2048,256]{1,0:T(8,128)(2,1)S(1)}, bf16[2048,256]{1,0:T(8,128)(2,1)}, u32[]{:S(2)}) copy-start(bf16[2048,256]{1,0:T(8,128)(2,1)} %weight.3) | copy-start | bytes 3145732
  24.4 55.2 %copy-start.7 = (f32[4,4,256]{2,1,0:T(4,128)S(1)}, f32[4,4,256]{2,1,0:T(4,128)}, u32[]{:S(2)}) copy-start(f32[4,4,256]{2,1,0:T(4,128)} %stream_in.1) | copy-start | bytes 49156
  24.4 55.2 %copy-start.9 = (f32[256]{0:T(256)S(1)}, f32[256]{0:T(256)}, u32[]{:S(2)}) copy-start(f32[256]{0:T(256)} %param.18) | copy-start | bytes 3076
  25.8 0.7 copy-start.4
  30.0 76.9 %copy-start = (bf16[2,52,16384]{2,1,0:T(8,128)(2,1)S(1)}, bf16[2,52,16384]{2,1,0:T(8,128)(2,1)}, u32[]{:S(2)}) copy-start(bf16[2,52,16384]{2,1,0:T(8,128)(2,1)} %copy.12.weight) | copy-start | bytes 10223620

commit v6 on v5

--- a/solution.py
+++ b/solution.py
@@ -63,10 +63,6 @@
     x = queries[...].astype(f32)
     x = jnp.concatenate([x[:, r, :] for r in range(ROWS)], axis=1).astype(bf16)
     out[...] = jnp.broadcast_to(x[None], out.shape)
-
-
-def tie(table, weight, out):
-    out[...] = table[...]
 
 
 def prepare(
@@ -157,7 +153,7 @@
     out[...] = block[...].astype(bf16)
 
 
-def finish(got, out):
+def finish(got, gate_up, out):
     n = got.shape[0]
     parts = got[...].astype(f32)
     flat = parts.reshape(n * 8, WIDTH)
@@ -248,9 +244,6 @@
     gathered = send(mine, ("z", "y"))
 
     drafted = drafted_key_value.transpose(0, 1, 3, 2, 4).reshape(COUNT, 2, WIDTH)
-    table = call(tie, shape(block_table.shape, jnp.int32), "vh", limit=62 * 2**20)(
-        block_table, gate_up
-    )
     bias, fresh_bias, fresh_keys, fresh_values, held = call(
         prepare,
         (
@@ -263,16 +256,16 @@
         "vsssvh",
         [dma((1,))],
         limit=8 * 2**20,
-    )(table, page_count, tail_fill, seq_index.reshape(1), drafted, paged_key_value)
+    )(block_table, page_count, tail_fill, seq_index.reshape(1), drafted, paged_key_value)
     block = call(
         attend,
         shape((seq_count, 2 * ROWS, WIDTH), bf16),
         "vvvvvv",
         [pltpu.VMEM((seq_count, 2 * ROWS, WIDTH), f32)],
     )(gathered, held, fresh_keys, fresh_values, bias, fresh_bias)
-    attended = call(finish, shape((seq_count, ROWS, WIDTH), bf16), "v")(
-        send(block, ("z", "y"))
-    )
+    attended = call(
+        finish, shape((seq_count, ROWS, WIDTH), bf16), "vh", limit=63_600_000
+    )(send(block, ("z", "y")), gate_up)
     partial_sum = call(project, shape((SIDE, COUNT, columns), bf16), "vv")(
         send(attended, ("z", "y")), out_weight
     )

time: 109 us -> 112 us (1.028)
  blocking collectives: 74 us -> 54.2 us
  waiting for transfers between devices: 2.87 us -> 13.2 us
  starting transfers between devices: 16.6 us -> 22.3 us
  local copies, waits for them, and re-layouts: 7.12 us -> 12.8 us
    all_to_all x4 -> x3, blocking collectives: 74 us -> 54.2 us  [send(): return lax.all_to_all(x, axis, split_axis=0, concat_axis=0, tiled=True)]
    all_to_all x1 -> x2, waiting for transfers between devices: 2.87 us -> 13.2 us  [send(): return lax.all_to_all(x, axis, split_axis=0, concat_axis=0, tiled=True)]
    all_to_all x1 -> x2, starting transfers between devices: 16.6 us -> 22.3 us  [send(): return lax.all_to_all(x, axis, split_axis=0, concat_axis=0, tiled=True)]
    unnamed x21 -> x23, local copies, waits for them, and re-layouts: 7.12 us -> 12.8 us
  transfers between devices with their start and end apart: 1 -> 2, of which waited for: 1 -> 2; matrix products, arithmetic and copies ran while one was open for 5% -> 5% of each run, Pallas kernels for 2% -> 1%
where the time goes in v6:
time: 112 us; the launch traced here: 111 us
  blocking collectives  54.2 us (48%)
  starting transfers between devices  22.3 us (20%)
  waiting for transfers between devices  13.2 us (12%)
  local copies, waits for them, and re-layouts  12.8 us (11%)
  Pallas kernels  8.28 us (7%)
    all_to_all x3, blocking collectives, send(): return lax.all_to_all(x, axis, split_axis=0, concat_axis=0, tiled=True)  54.2 us
    all_to_all x2, starting transfers between devices, send(): return lax.all_to_all(x, axis, split_axis=0, concat_axis=0, tiled=True)  22.3 us
    all_to_all x2, waiting for transfers between devices, send(): return lax.all_to_all(x, axis, split_axis=0, concat_axis=0, tiled=True)  13.2 us
    unnamed x23, local copies, waits for them, and re-layouts  12.8 us
  transfers between devices with their start and end apart: 2, of which 2 were waited for; matrix products, arithmetic and copies ran while one was open for 5% of the time, Pallas kernels for 1%

profile of v6, /device:TPU:8, one launch (start us, length us, event | category | flops | bytes accessed | tf_op | source)
XLA Modules:
  0.0 111.5 jit_solution(12092529271166369710)
XLA Ops:
  0.6 0.0 copy-start.8
  0.6 0.7 copy-done.8
  1.3 0.7 shard_map.113
  2.0 16.6 %all-to-all-start = ((bf16[64,4,128]{2,1,0:T(4,128)(2,1)}), bf16[64,4,128]{2,1,0:T(4,128)(2,1)S(1)}, u32[]{:S(2)}, u32[]{:S(2)}) async-start(bf16[64,4,128]{2,1,0:T(4,128)(2,1)} %shard_map.113), calls=%async_computation | async-start | bytes 131072 | tf_op jit(solution)/shard_map/all_to_all | solution.py:220
  18.6 0.0 copy-start.2
  18.6 1.0 copy-done.2
  19.7 0.0 copy-start.3
  19.7 0.7 copy-done.3
  20.4 0.0 copy-start.4
  20.4 0.7 copy-done.4
  21.1 0.0 copy-start.5
  21.1 0.7 copy-done.5
  21.7 0.0 copy-start.6
  21.7 0.7 copy-done.6
  22.4 0.7 shard_map.114
  23.1 7.0 %all-to-all-done.gathered = bf16[64,4,128]{2,1,0:T(4,128)(2,1)S(1)} async-done(((bf16[64,4,128]{2,1,0:T(4,128)(2,1)}), bf16[64,4,128]{2,1,0:T(4,128)(2,1)S(1)}, u32[]{:S(2)}, u32[]{:S(2)}) %all-to-all-start) | async-done | bytes 65568 | tf_op jit(solution)/shard_map/all_to_all | solution.py:220
  30.0 2.1 %shard_map.115 = bf16[64,8,128]{2,1,0:T(8,128)(2,1)} custom-call(bf16[64,4,128]{2,1,0:T(4,128)(2,1)S(1)} %all-to-all-done.gathered, bf16[2,1,8,128,128]{4,3,2,1,0:T(8,128)(2,1)S(1)} %get-tuple-element.9.paged, bf16[16,128]{1,0:T(8,128)(2,1)S(1)} %get-tuple-element.10.fresh_keys, bf16[16,128]{1,0:T(8,128)(2,1)S(1)} %get-tuple-element.11.fresh_values, ...), custom_call_target="tpu_custom_call" | custom-call | flops 67108864 | bytes 16777216 | tf_op jit(solution)/shard_map/pallas_call | solution.py:260
  32.1 5.8 %all-to-all-start.1 = ((bf16[64,8,128]{2,1,0:T(8,128)(2,1)}), bf16[64,8,128]{2,1,0:T(8,128)(2,1)S(1)}, u32[]{:S(2)}, u32[]{:S(2)}) async-start(bf16[64,8,128]{2,1,0:T(8,128)(2,1)} %shard_map.115), calls=%async_computation.1 | async-start | bytes 262144 | tf_op jit(solution)/shard_map/all_to_all | solution.py:220
  37.8 5.7 %copy.12.gate_up.weight = bf16[2,52,16384]{2,1,0:T(8,128)(2,1)} copy(bf16[2,52,16384]{2,0,1:T(2,128)(2,1)} %param.19) | data formatting | bytes 6815744 | tf_op args[9]
  43.5 6.2 %all-to-all-done.1.got = bf16[64,8,128]{2,1,0:T(8,128)(2,1)S(1)} async-done(((bf16[64,8,128]{2,1,0:T(8,128)(2,1)}), bf16[64,8,128]{2,1,0:T(8,128)(2,1)S(1)}, u32[]{:S(2)}, u32[]{:S(2)}) %all-to-all-start.1) | async-done | bytes 131104 | tf_op jit(solution)/shard_map/all_to_all | solution.py:220
  49.7 0.6 copy-done.10
  50.4 1.9 %shard_map.116 = bf16[64,4,128]{2,1,0:T(4,128)(2,1)} custom-call(bf16[64,8,128]{2,1,0:T(8,128)(2,1)} %copy-done.10, bf16[2,52,16384]{2,1,0:T(8,128)(2,1)} %copy.12.gate_up.weight), custom_call_target="tpu_custom_call" | custom-call | flops 67108864 | bytes 16777216 | tf_op jit(solution)/shard_map/pallas_call | solution.py:266
  52.3 17.8 %all_to_all.25.attended = bf16[64,4,128]{2,1,0:T(4,128)(2,1)S(1)} all-to-all(bf16[64,4,128]{2,1,0:T(4,128)(2,1)} %shard_map.116), channel_id=1, replica_groups=mesh['x'=4,'core'=2,'z'=8,'y'=8] {'z','y'}, dimensions={0} | all-to-all | bytes 131072 | tf_op jit(solution)/shard_map/all_to_all | solution.py:220
  70.1 0.0 copy-done.1
  70.1 0.5 shard_map.117
  70.6 9.7 %all_to_all.26.parts = bf16[8,16,256]{2,1,0:T(8,128)(2,1)S(1)} all-to-all(bf16[8,16,256]{2,1,0:T(8,128)(2,1)S(1)} %shard_map.117), channel_id=1, replica_groups=mesh['x'=4,'core'=2,'z'=8,'y'=8] {'x','core'}, dimensions={0} | all-to-all | bytes 131072 | tf_op jit(solution)/shard_map/all_to_all | solution.py:220
  80.3 0.0 copy-done.7
  80.4 0.0 copy-done.9
  80.4 0.6 shard_map.118
  81.0 26.6 %all_to_all.27.got = bf16[64,40,128]{2,1,0:T(8,128)(2,1)S(1)} all-to-all(bf16[64,40,128]{2,1,0:T(8,128)(2,1)S(1)} %get-tuple-element.14), channel_id=1, replica_groups=mesh['x'=4,'core'=2,'z'=8,'y'=8] {'z','y'}, dimensions={0} | all-to-all | bytes 1310720 | tf_op jit(solution)/shard_map/all_to_all | solution.py:220
  107.6 2.0 %copy-done = bf16[2,52,16384]{2,1,0:T(8,128)(2,1)S(1)} copy-done((bf16[2,52,16384]{2,1,0:T(8,128)(2,1)S(1)}, bf16[2,52,16384]{2,1,0:T(8,128)(2,1)}, u32[]{:S(2)}) %copy-start) | copy-done | bytes 3407896
  109.6 1.8 %shard_map.119 = bf16[4,4,52]{2,1,0:T(4,128)(2,1)} custom-call(bf16[64,40,128]{2,1,0:T(8,128)(2,1)S(1)} %all_to_all.27.got, bf16[2,52,16384]{2,1,0:T(8,128)(2,1)S(1)} %copy-done), custom_call_target="tpu_custom_call" | custom-call | flops 67108864 | bytes 16777216 | tf_op jit(solution)/shard_map/pallas_call | solution.py:278
  (5 shorter events, 0.0 us)
Async XLA Ops:
  0.6 0.7 copy-start.8
  2.0 28.0 %all-to-all-start = ((bf16[64,4,128]{2,1,0:T(4,128)(2,1)}), bf16[64,4,128]{2,1,0:T(4,128)(2,1)S(1)}, u32[]{:S(2)}, u32[]{:S(2)}) async-start(bf16[64,4,128]{2,1,0:T(4,128)(2,1)} %shard_map.113), calls=%async_computation | async-start | bytes 131072 | tf_op jit(solution)/shard_map/all_to_all | solution.py:220
  18.6 1.0 copy-start.2
  19.7 0.7 copy-start.3
  20.4 0.7 copy-start.4
  21.1 0.7 copy-start.5
  21.7 0.7 copy-start.6
  32.1 17.7 %all-to-all-start.1 = ((bf16[64,8,128]{2,1,0:T(8,128)(2,1)}), bf16[64,8,128]{2,1,0:T(8,128)(2,1)S(1)}, u32[]{:S(2)}, u32[]{:S(2)}) async-start(bf16[64,8,128]{2,1,0:T(8,128)(2,1)} %shard_map.115), calls=%async_computation.1 | async-start | bytes 262144 | tf_op jit(solution)/shard_map/all_to_all | solution.py:220
  43.5 26.6 %copy-start.1 = (bf16[2048,256]{1,0:T(8,128)(2,1)S(1)}, bf16[2048,256]{1,0:T(8,128)(2,1)}, u32[]{:S(2)}) copy-start(bf16[2048,256]{1,0:T(8,128)(2,1)} %weight.2) | copy-start | bytes 3145732
  43.5 36.9 %copy-start.7 = (f32[4,4,256]{2,1,0:T(4,128)S(1)}, f32[4,4,256]{2,1,0:T(4,128)}, u32[]{:S(2)}) copy-start(f32[4,4,256]{2,1,0:T(4,128)} %stream_in.1) | copy-start | bytes 49156
  43.5 36.9 %copy-start.9 = (f32[256]{0:T(256)S(1)}, f32[256]{0:T(256)}, u32[]{:S(2)}) copy-start(f32[256]{0:T(256)} %param.18) | copy-start | bytes 3076
  49.7 0.6 copy-start.10
  107.6 2.0 %copy-start = (bf16[2,52,16384]{2,1,0:T(8,128)(2,1)S(1)}, bf16[2,52,16384]{2,1,0:T(8,128)(2,1)}, u32[]{:S(2)}) copy-start(bf16[2,52,16384]{2,1,0:T(8,128)(2,1)} %copy.12.gate_up.weight) | copy-start | bytes 10223620

commit v7 on v5

--- a/solution.py
+++ b/solution.py
@@ -14,6 +14,7 @@
 ROWS = 4
 COUNT = STEPS * ROWS
 QUARTER = 32
+PAGES = 8
 SIDE = 8
 
 low = -1e30
@@ -65,15 +66,9 @@
     out[...] = jnp.broadcast_to(x[None], out.shape)
 
 
-def tie(table, weight, out):
-    out[...] = table[...]
-
-
-def prepare(
-    table, count, tail, index, drafted, paged, bias, fresh_bias, fresh_keys, fresh_values, held, sems
-):
-    moves = begin([(paged, held)], sems)
-    pages, page_len = paged.shape[2], paged.shape[3]
+def prepare(table, count, tail, index, drafted, bias, fresh_keys, fresh_values):
+    pages = PAGES
+    page_len = bias.shape[1] // pages
     row, page = iota(table.shape, 0), iota(table.shape, 1)
     counts = tails = jnp.zeros(table.shape, jnp.int32)
     for r in range(ROWS):
@@ -87,28 +82,12 @@
         filled = jnp.where(slots == index[0] * pages + p, fill, 0.0)
         filled = jnp.max(filled, axis=1, keepdims=True)
         bias[:, p * page_len : (p + 1) * page_len] = jnp.where(token < filled, 0.0, low)
-    step = iota((GROUP * STEPS, COUNT), 0) % STEPS
-    key = iota((GROUP * STEPS, COUNT), 1)
-    causal = key // ROWS <= step
-    for r in range(ROWS):
-        ok = causal & (key % ROWS == r) & (index[0] == r)
-        fresh_bias[r] = jnp.where(ok, 0.0, low)
     both = drafted[...].astype(f32)
     fresh_keys[...] = both[:, 0, :].astype(bf16)
     fresh_values[...] = both[:, 1, :].astype(bf16)
-    moves[0].wait()
-
-
-def attend(
-    gathered,
-    paged,
-    fresh_keys,
-    fresh_values,
-    bias,
-    fresh_bias,
-    out,
-    block,
-):
+
+
+def attend(gathered, paged, fresh_keys, fresh_values, bias, index, out, block):
     sent = jnp.concatenate([gathered[:, i, :].astype(f32) for i in range(STEPS)], axis=0)
     shape = (STEPS * GROUP * 4, WIDTH)
     quarter = iota(shape, 0) % 4
@@ -135,10 +114,12 @@
     fresh_v = jnp.concatenate([fresh_v, jnp.ones(fresh_v.shape, bf16)], axis=1)
     each = GROUP * STEPS
     masks = [jnp.broadcast_to(bias[r : r + 1, :], (each, bias.shape[1])) for r in range(ROWS)]
-    fresh_masks = [fresh_bias[r] for r in range(ROWS)]
+    query_at, key_at = iota((ROWS * each, COUNT), 0), iota((ROWS * each, COUNT), 1)
+    ok = (key_at % ROWS == query_at // each) & (key_at // ROWS <= query_at % STEPS)
+    ok = ok & (query_at // each == index[0])
     scale = WIDTH ** (-0.5)
     scores = dot_t(query, keys) * scale + jnp.concatenate(masks, axis=0)
-    fresh = dot_t(query, fresh_keys[...]) * scale + jnp.concatenate(fresh_masks, axis=0)
+    fresh = jnp.where(ok, dot_t(query, fresh_keys[...]) * scale, low)
     peak = jnp.maximum(
         jnp.max(scores, axis=1, keepdims=True), jnp.max(fresh, axis=1, keepdims=True)
     )
@@ -202,22 +183,20 @@
     out[...] = jnp.broadcast_to(block[None], out.shape)
 
 
-def feed(got, weight, out):
+def lay(got, tokens, inverse):
     n = got.shape[0]
-    tokens = jnp.concatenate(
-        [got[s, COUNT * j : COUNT * (j + 1), :] for s in range(n) for j in range(2)], axis=1
-    )
+    for s in range(n):
+        for j in range(2):
+            at = (2 * s + j) * WIDTH
+            tokens[:, at : at + WIDTH] = got[s, COUNT * j : COUNT * (j + 1), :]
     stats = jnp.sum(got[:, 32:40, :].astype(f32), axis=0)
     stats = jnp.concatenate([stats, stats], axis=0)
     at = iota((COUNT, WIDTH), 1) - iota((COUNT, WIDTH), 0)
     stats = jnp.where((at == 0) | (at == 32) | (at == 64), stats, 0.0)
     squares = jnp.sum(stats, axis=1, keepdims=True)
-    inverse = lax.rsqrt(squares / (n * 2 * WIDTH) + epsilon)
-    gate = dot_t(tokens, weight[0]) * inverse
-    up = dot_t(tokens, weight[1]) * inverse
-    hidden = gate / (1.0 + jnp.exp(-gate)) * up
-    for i in range(STEPS):
-        out[i] = hidden[ROWS * i : ROWS * (i + 1)].astype(bf16)
+    inverse[...] = jnp.broadcast_to(
+        lax.rsqrt(squares / (n * 2 * WIDTH) + epsilon), inverse.shape
+    )
 
 
 def send(x, axis):
@@ -248,28 +227,23 @@
     gathered = send(mine, ("z", "y"))
 
     drafted = drafted_key_value.transpose(0, 1, 3, 2, 4).reshape(COUNT, 2, WIDTH)
-    table = call(tie, shape(block_table.shape, jnp.int32), "vh", limit=62 * 2**20)(
-        block_table, gate_up
-    )
-    bias, fresh_bias, fresh_keys, fresh_values, held = call(
+    index = seq_index.reshape(1)
+    bias, fresh_keys, fresh_values = call(
         prepare,
         (
             shape((ROWS, pages * page_len), f32),
-            shape((ROWS, GROUP * STEPS, COUNT), f32),
             shape((COUNT, WIDTH), bf16),
             shape((COUNT, WIDTH), bf16),
-            shape(paged_key_value.shape, bf16),
         ),
-        "vsssvh",
-        [dma((1,))],
+        "vsssv",
         limit=8 * 2**20,
-    )(table, page_count, tail_fill, seq_index.reshape(1), drafted, paged_key_value)
+    )(block_table, page_count, tail_fill, index, drafted)
     block = call(
         attend,
         shape((seq_count, 2 * ROWS, WIDTH), bf16),
-        "vvvvvv",
+        "vvvvvs",
         [pltpu.VMEM((seq_count, 2 * ROWS, WIDTH), f32)],
-    )(gathered, held, fresh_keys, fresh_values, bias, fresh_bias)
+    )(gathered, paged_key_value, fresh_keys, fresh_values, bias, index)
     attended = call(finish, shape((seq_count, ROWS, WIDTH), bf16), "v")(
         send(block, ("z", "y"))
     )
@@ -282,9 +256,15 @@
         "vvv",
         [pltpu.VMEM((COUNT, columns), f32)],
     )(send(partial_sum, ("x", "core")), stream_in, norm_gain.reshape(1, columns))
-    hidden = call(feed, shape((STEPS, ROWS, units), bf16), "vv")(
-        send(scaled, ("z", "y")), gate_up
-    )
+    tokens, inverse = call(
+        lay,
+        (shape((COUNT, seq_count * columns), bf16), shape((COUNT, WIDTH), f32)),
+        "v",
+    )(send(scaled, ("z", "y")))
+    both = jnp.einsum("nc,kfc->knf", tokens, gate_up, preferred_element_type=f32)
+    both = both * inverse[None, :, :units]
+    hidden = both[0] / (1.0 + jnp.exp(-both[0])) * both[1]
+    hidden = hidden.astype(bf16).reshape(STEPS, ROWS, units)
     return hidden, stream
 
 

time: 109 us -> 108 us (level)
  waiting for transfers between devices: 2.87 us -> 8.05 us
  blocking collectives: 74 us -> 68.9 us
  Pallas kernels: 7.43 us -> 4.39 us
  matrix products: 0 us -> 2 us
  local copies, waits for them, and re-layouts: 7.12 us -> 5.81 us
    all_to_all x1, waiting for transfers between devices: 2.87 us -> 8.05 us  [send(): return lax.all_to_all(x, axis, split_axis=0, concat_axis=0, tiled=True)]
    all_to_all x4, blocking collectives: 74 us -> 68.9 us  [send(): return lax.all_to_all(x, axis, split_axis=0, concat_axis=0, tiled=True)]
    pallas_call x4 -> x3, Pallas kernels: 5.24 us -> 2.2 us  [the longest x1 1.42 us: shards(): call(attend, shape((seq_count, 2 * ROWS, WIDTH), bf16), 'vvvvvs', [pltpu....]
    dot_general x0 -> x1, matrix products: none -> 2 us  [shards(): jnp.einsum('nc,kfc->knf', tokens, gate_up, preferred_element_type=f32)]
    unnamed x21 -> x20, local copies, waits for them, and re-layouts: 7.12 us -> 5.8 us
  transfers between devices with their start and end apart: 1 -> 1, of which waited for: 1 -> 1; matrix products, arithmetic and copies ran while one was open for 5% -> 0% of each run, Pallas kernels for 2% -> 1%
where the time goes in v7:
time: 108 us; the launch traced here: 107 us
  blocking collectives  68.9 us (64%)
  starting transfers between devices  16.6 us (15%)
  waiting for transfers between devices  8.05 us (7%)
  local copies, waits for them, and re-layouts  5.81 us (5%)
  Pallas kernels  4.39 us (4%)
  matrix products  2 us (2%)
    all_to_all x4, blocking collectives, send(): return lax.all_to_all(x, axis, split_axis=0, concat_axis=0, tiled=True)  68.9 us
    all_to_all x1, starting transfers between devices, send(): return lax.all_to_all(x, axis, split_axis=0, concat_axis=0, tiled=True)  16.6 us
    all_to_all x1, waiting for transfers between devices, send(): return lax.all_to_all(x, axis, split_axis=0, concat_axis=0, tiled=True)  8.05 us
    unnamed x20, local copies, waits for them, and re-layouts  5.8 us
  transfers between devices with their start and end apart: 1, of which 1 were waited for; matrix products, arithmetic and copies ran while one was open for 0% of the time, Pallas kernels for 1%

profile of v7, /device:TPU:8, one launch (start us, length us, event | category | flops | bytes accessed | tf_op | source)
XLA Modules:
  0.0 107.1 jit_solution(7365483192051093389)
XLA Ops:
  0.6 0.0 copy-start
  0.6 0.0 copy-start.3
  0.7 0.0 copy-start.5
  0.7 0.8 copy-done.5
  1.5 0.0 copy-start.7
  1.5 0.7 shard_map.113
  2.2 16.6 %all-to-all-start = ((bf16[64,4,128]{2,1,0:T(4,128)(2,1)}), bf16[64,4,128]{2,1,0:T(4,128)(2,1)S(1)}, u32[]{:S(2)}, u32[]{:S(2)}) async-start(bf16[64,4,128]{2,1,0:T(4,128)(2,1)} %shard_map.113), calls=%async_computation | async-start | bytes 131072 | tf_op jit(solution)/shard_map/all_to_all | solution.py:203
  18.8 0.0 copy-start.4
  18.8 0.7 copy-done.4
  19.5 0.0 copy-start.6
  19.5 0.7 copy-done.6
  20.2 0.0 copy-start.8
  20.2 0.7 copy-done.8
  20.8 0.7 copy-done.9
  21.5 0.6 shard_map.114
  22.1 8.0 %all-to-all-done.gathered = bf16[64,4,128]{2,1,0:T(4,128)(2,1)S(1)} async-done(((bf16[64,4,128]{2,1,0:T(4,128)(2,1)}), bf16[64,4,128]{2,1,0:T(4,128)(2,1)S(1)}, u32[]{:S(2)}, u32[]{:S(2)}) %all-to-all-start) | async-done | bytes 65568 | tf_op jit(solution)/shard_map/all_to_all | solution.py:203
  30.2 1.0 copy-done.2
  31.2 1.4 %shard_map.115 = bf16[64,8,128]{2,1,0:T(8,128)(2,1)S(1)} custom-call(bf16[64,4,128]{2,1,0:T(4,128)(2,1)S(1)} %all-to-all-done.gathered, bf16[2,1,8,128,128]{4,3,2,1,0:T(8,128)(2,1)S(1)} %copy-done.2, bf16[16,128]{1,0:T(8,128)(2,1)S(1)} %get-tuple-element.9.fresh_keys, bf16[16,128]{1,0:T(8,128)(2,1)S(1)} %get-tuple-element.10.fresh_values, ...), custom_call_target="tpu_custom_call" | custom-call | flops 67108864 | bytes 16777216 | tf_op jit(solution)/shard_map/pallas_call | solution.py:241
  32.7 16.5 %all_to_all.25.got = bf16[64,8,128]{2,1,0:T(8,128)(2,1)S(1)} all-to-all(bf16[64,8,128]{2,1,0:T(8,128)(2,1)S(1)} %shard_map.115), channel_id=1, replica_groups=mesh['x'=4,'core'=2,'z'=8,'y'=8] {'z','y'}, dimensions={0} | all-to-all | bytes 262144 | tf_op jit(solution)/shard_map/all_to_all | solution.py:203
  49.2 0.3 shard_map.116
  49.5 16.0 %all_to_all.26.attended = bf16[64,4,128]{2,1,0:T(4,128)(2,1)S(1)} all-to-all(bf16[64,4,128]{2,1,0:T(4,128)(2,1)S(1)} %shard_map.116), channel_id=1, replica_groups=mesh['x'=4,'core'=2,'z'=8,'y'=8] {'z','y'}, dimensions={0} | all-to-all | bytes 131072 | tf_op jit(solution)/shard_map/all_to_all | solution.py:203
  65.5 1.2 %copy-done.1 = bf16[2048,256]{1,0:T(8,128)(2,1)S(1)} copy-done((bf16[2048,256]{1,0:T(8,128)(2,1)S(1)}, bf16[2048,256]{1,0:T(8,128)(2,1)}, u32[]{:S(2)}) %copy-start.1) | copy-done | bytes 1048600
  66.8 0.5 shard_map.117
  67.3 9.7 %all_to_all.27.parts = bf16[8,16,256]{2,1,0:T(8,128)(2,1)S(1)} all-to-all(bf16[8,16,256]{2,1,0:T(8,128)(2,1)S(1)} %shard_map.117), channel_id=1, replica_groups=mesh['x'=4,'core'=2,'z'=8,'y'=8] {'x','core'}, dimensions={0} | all-to-all | bytes 131072 | tf_op jit(solution)/shard_map/all_to_all | solution.py:203
  77.0 0.0 copy-done.3
  77.0 0.0 copy-done.7
  77.0 0.6 shard_map.118
  77.6 26.6 %all_to_all.28.got = bf16[64,40,128]{2,1,0:T(8,128)(2,1)S(1)} all-to-all(bf16[64,40,128]{2,1,0:T(8,128)(2,1)S(1)} %get-tuple-element.12), channel_id=1, replica_groups=mesh['x'=4,'core'=2,'z'=8,'y'=8] {'z','y'}, dimensions={0} | all-to-all | bytes 1310720 | tf_op jit(solution)/shard_map/all_to_all | solution.py:203
  104.3 0.2 shard_map.119
  104.4 0.0 copy-done
  104.4 2.0 %fusion.5 = f32[2,16,52]{2,1,0:T(8,128)S(1)} fusion(bf16[2,52,16384]{2,0,1:T(2,128)(2,1)S(1)} %copy-done, bf16[16,16384]{1,0:T(8,128)(2,1)S(1)} %get-tuple-element.13, f32[16,52]{1,0:T(8,128)S(1)} %bitcast.12), kind=kOutput, calls=%fused_computation.3 | convolution fusion | flops 54527616 | bytes 3942144 | tf_op jit(solution)/shard_map/nc,kfc->knf/dot_general | solution.py:264
  106.5 0.6 multiply_convert_fusion
  (4 shorter events, 0.0 us)
Async XLA Ops:
  0.6 103.8 %copy-start = (bf16[2,52,16384]{2,0,1:T(2,128)(2,1)S(1)}, bf16[2,52,16384]{2,0,1:T(2,128)(2,1)}, u32[]{:S(2)}) copy-start(bf16[2,52,16384]{2,0,1:T(2,128)(2,1)} %param.19) | copy-start | bytes 10223620
  0.6 76.4 %copy-start.3 = (f32[4,4,256]{2,1,0:T(4,128)S(1)}, f32[4,4,256]{2,1,0:T(4,128)}, u32[]{:S(2)}) copy-start(f32[4,4,256]{2,1,0:T(4,128)} %stream_in.1) | copy-start | bytes 49156
  0.7 0.8 copy-start.5
  1.5 75.5 %copy-start.7 = (f32[256]{0:T(256)S(1)}, f32[256]{0:T(256)}, u32[]{:S(2)}) copy-start(f32[256]{0:T(256)} %param.18) | copy-start | bytes 3076
  2.2 28.0 %all-to-all-start = ((bf16[64,4,128]{2,1,0:T(4,128)(2,1)}), bf16[64,4,128]{2,1,0:T(4,128)(2,1)S(1)}, u32[]{:S(2)}, u32[]{:S(2)}) async-start(bf16[64,4,128]{2,1,0:T(4,128)(2,1)} %shard_map.113), calls=%async_computation | async-start | bytes 131072 | tf_op jit(solution)/shard_map/all_to_all | solution.py:203
  18.8 0.7 copy-start.4
  19.5 0.7 copy-start.6
  20.2 0.7 copy-start.8
  20.8 0.7 copy-start.9
  30.2 1.0 copy-start.2
  65.5 1.2 %copy-start.1 = (bf16[2048,256]{1,0:T(8,128)(2,1)S(1)}, bf16[2048,256]{1,0:T(8,128)(2,1)}, u32[]{:S(2)}) copy-start(bf16[2048,256]{1,0:T(8,128)(2,1)} %weight.1) | copy-start | bytes 3145732

commit v8 on v7

--- a/solution.py
+++ b/solution.py
@@ -51,13 +51,6 @@
         cost_estimate=pl.CostEstimate(flops=2**26, bytes_accessed=moved, transcendentals=2**18),
         compiler_params=pltpu.CompilerParams(vmem_limit_bytes=limit),
     )
-
-
-def begin(pairs, sems):
-    moves = [pltpu.make_async_copy(a, b, sems.at[i]) for i, (a, b) in enumerate(pairs)]
-    for move in moves:
-        move.start()
-    return moves
 
 
 def copies(queries, out):
@@ -87,7 +80,11 @@
     fresh_values[...] = both[:, 1, :].astype(bf16)
 
 
-def attend(gathered, paged, fresh_keys, fresh_values, bias, index, out, block):
+def attend(
+    gathered, paged, fresh_keys, fresh_values, bias, index, out_weight, out, held, block, sems
+):
+    move = pltpu.make_async_copy(out_weight, held, sems.at[0])
+    move.start()
     sent = jnp.concatenate([gathered[:, i, :].astype(f32) for i in range(STEPS)], axis=0)
     shape = (STEPS * GROUP * 4, WIDTH)
     quarter = iota(shape, 0) % 4
@@ -136,6 +133,7 @@
         block[:, r, :] = mean[r * each : (r + 1) * each]
         block[:, ROWS + r, :] = stat[r * each : (r + 1) * each]
     out[...] = block[...].astype(bf16)
+    move.wait()
 
 
 def finish(got, out):
@@ -222,7 +220,6 @@
     units = gate_up.shape[1]
 
     shape = jax.ShapeDtypeStruct
-    dma = pltpu.SemaphoreType.DMA
     mine = call(copies, shape((seq_count, STEPS, ROWS * QUARTER), bf16), "v")(queries)
     gathered = send(mine, ("z", "y"))
 
@@ -238,17 +235,17 @@
         "vsssv",
         limit=8 * 2**20,
     )(block_table, page_count, tail_fill, index, drafted)
-    block = call(
+    block, weight = call(
         attend,
-        shape((seq_count, 2 * ROWS, WIDTH), bf16),
-        "vvvvvs",
-        [pltpu.VMEM((seq_count, 2 * ROWS, WIDTH), f32)],
-    )(gathered, paged_key_value, fresh_keys, fresh_values, bias, index)
+        (shape((seq_count, 2 * ROWS, WIDTH), bf16), shape(out_weight.shape, bf16)),
+        "vvvvvsh",
+        [pltpu.VMEM((seq_count, 2 * ROWS, WIDTH), f32), pltpu.SemaphoreType.DMA((1,))],
+    )(gathered, paged_key_value, fresh_keys, fresh_values, bias, index, out_weight)
     attended = call(finish, shape((seq_count, ROWS, WIDTH), bf16), "v")(
         send(block, ("z", "y"))
     )
     partial_sum = call(project, shape((SIDE, COUNT, columns), bf16), "vv")(
-        send(attended, ("z", "y")), out_weight
+        send(attended, ("z", "y")), weight
     )
     scaled, stream = call(
         normalise,

time: 108 us -> 108 us (level)
  no operation moved by 1% of the time
where the time goes in v8:
time: 108 us; the launch traced here: 107 us
  blocking collectives  68.9 us (64%)
  starting transfers between devices  16.6 us (15%)
  waiting for transfers between devices  8.05 us (7%)
  local copies, waits for them, and re-layouts  5.81 us (5%)
  Pallas kernels  4.47 us (4%)
  matrix products  2 us (2%)
    all_to_all x4, blocking collectives, send(): return lax.all_to_all(x, axis, split_axis=0, concat_axis=0, tiled=True)  68.9 us
    all_to_all x1, starting transfers between devices, send(): return lax.all_to_all(x, axis, split_axis=0, concat_axis=0, tiled=True)  16.6 us
    all_to_all x1, waiting for transfers between devices, send(): return lax.all_to_all(x, axis, split_axis=0, concat_axis=0, tiled=True)  8.05 us
    unnamed x20, local copies, waits for them, and re-layouts  5.8 us
  transfers between devices with their start and end apart: 1, of which 1 were waited for; matrix products, arithmetic and copies ran while one was open for 0% of the time, Pallas kernels for 1%

profile of v8, /device:TPU:8, one launch (start us, length us, event | category | flops | bytes accessed | tf_op | source)
XLA Modules:
  0.0 107.2 jit_solution(15730500846345121462)
XLA Ops:
  0.6 0.0 copy-start
  0.6 0.0 copy-start.3
  0.7 0.0 copy-start.5
  0.7 0.8 copy-done.5
  1.5 0.0 copy-start.7
  1.5 0.7 shard_map.113
  2.2 16.6 %all-to-all-start = ((bf16[64,4,128]{2,1,0:T(4,128)(2,1)}), bf16[64,4,128]{2,1,0:T(4,128)(2,1)S(1)}, u32[]{:S(2)}, u32[]{:S(2)}) async-start(bf16[64,4,128]{2,1,0:T(4,128)(2,1)} %shard_map.113), calls=%async_computation | async-start | bytes 131072 | tf_op jit(solution)/shard_map/all_to_all | solution.py:201
  18.8 0.0 copy-start.4
  18.8 0.7 copy-done.4
  19.5 0.0 copy-start.6
  19.5 0.7 copy-done.6
  20.2 0.0 copy-start.8
  20.2 0.7 copy-done.8
  20.9 0.7 copy-done.9
  21.5 0.6 shard_map.114
  22.1 8.0 %all-to-all-done.gathered = bf16[64,4,128]{2,1,0:T(4,128)(2,1)S(1)} async-done(((bf16[64,4,128]{2,1,0:T(4,128)(2,1)}), bf16[64,4,128]{2,1,0:T(4,128)(2,1)S(1)}, u32[]{:S(2)}, u32[]{:S(2)}) %all-to-all-start) | async-done | bytes 65568 | tf_op jit(solution)/shard_map/all_to_all | solution.py:201
  30.2 1.2 %copy-done.1 = bf16[2048,256]{1,0:T(8,128)(2,1)S(1)} copy-done((bf16[2048,256]{1,0:T(8,128)(2,1)S(1)}, bf16[2048,256]{1,0:T(8,128)(2,1)}, u32[]{:S(2)}) %copy-start.1) | copy-done | bytes 1048600
  31.4 1.0 copy-done.2
  32.5 1.5 %shard_map.115 = (bf16[64,8,128]{2,1,0:T(8,128)(2,1)S(1)}, bf16[2048,256]{1,0:T(8,128)(2,1)S(1)}) custom-call(bf16[64,4,128]{2,1,0:T(4,128)(2,1)S(1)} %all-to-all-done.gathered, bf16[2,1,8,128,128]{4,3,2,1,0:T(8,128)(2,1)S(1)} %copy-done.2, bf16[16,128]{1,0:T(8,128)(2,1)S(1)} %get-tuple-element.11.fresh_keys, ...), custom_call_target="tpu_custom_call" | custom-call | flops 67108864 | bytes 16777216 | tf_op jit(solution)/shard_map/pallas_call | solution.py:238
  34.0 16.5 %all_to_all.25.got = bf16[64,8,128]{2,1,0:T(8,128)(2,1)S(1)} all-to-all(bf16[64,8,128]{2,1,0:T(8,128)(2,1)S(1)} %get-tuple-element.14), channel_id=1, replica_groups=mesh['x'=4,'core'=2,'z'=8,'y'=8] {'z','y'}, dimensions={0} | all-to-all | bytes 262144 | tf_op jit(solution)/shard_map/all_to_all | solution.py:201
  50.5 0.3 shard_map.116
  50.8 16.0 %all_to_all.26.attended = bf16[64,4,128]{2,1,0:T(4,128)(2,1)S(1)} all-to-all(bf16[64,4,128]{2,1,0:T(4,128)(2,1)S(1)} %shard_map.116), channel_id=1, replica_groups=mesh['x'=4,'core'=2,'z'=8,'y'=8] {'z','y'}, dimensions={0} | all-to-all | bytes 131072 | tf_op jit(solution)/shard_map/all_to_all | solution.py:201
  66.9 0.5 shard_map.117
  67.4 9.7 %all_to_all.27.parts = bf16[8,16,256]{2,1,0:T(8,128)(2,1)S(1)} all-to-all(bf16[8,16,256]{2,1,0:T(8,128)(2,1)S(1)} %shard_map.117), channel_id=1, replica_groups=mesh['x'=4,'core'=2,'z'=8,'y'=8] {'x','core'}, dimensions={0} | all-to-all | bytes 131072 | tf_op jit(solution)/shard_map/all_to_all | solution.py:201
  77.1 0.0 copy-done.3
  77.1 0.0 copy-done.7
  77.1 0.6 shard_map.118
  77.7 26.6 %all_to_all.28.got = bf16[64,40,128]{2,1,0:T(8,128)(2,1)S(1)} all-to-all(bf16[64,40,128]{2,1,0:T(8,128)(2,1)S(1)} %get-tuple-element.16), channel_id=1, replica_groups=mesh['x'=4,'core'=2,'z'=8,'y'=8] {'z','y'}, dimensions={0} | all-to-all | bytes 1310720 | tf_op jit(solution)/shard_map/all_to_all | solution.py:201
  104.4 0.2 shard_map.119
  104.5 0.0 copy-done
  104.5 2.0 %fusion.5 = f32[2,16,52]{2,1,0:T(8,128)S(1)} fusion(bf16[2,52,16384]{2,0,1:T(2,128)(2,1)S(1)} %copy-done, bf16[16,16384]{1,0:T(8,128)(2,1)S(1)} %get-tuple-element.17, f32[16,52]{1,0:T(8,128)S(1)} %bitcast.12), kind=kOutput, calls=%fused_computation.3 | convolution fusion | flops 54527616 | bytes 3942144 | tf_op jit(solution)/shard_map/nc,kfc->knf/dot_general | solution.py:261
  106.5 0.6 multiply_convert_fusion
  (4 shorter events, 0.0 us)
Async XLA Ops:
  0.6 103.9 %copy-start = (bf16[2,52,16384]{2,0,1:T(2,128)(2,1)S(1)}, bf16[2,52,16384]{2,0,1:T(2,128)(2,1)}, u32[]{:S(2)}) copy-start(bf16[2,52,16384]{2,0,1:T(2,128)(2,1)} %param.19) | copy-start | bytes 10223620
  0.6 76.5 %copy-start.3 = (f32[4,4,256]{2,1,0:T(4,128)S(1)}, f32[4,4,256]{2,1,0:T(4,128)}, u32[]{:S(2)}) copy-start(f32[4,4,256]{2,1,0:T(4,128)} %stream_in.1) | copy-start | bytes 49156
  0.7 0.8 copy-start.5
  1.5 75.6 %copy-start.7 = (f32[256]{0:T(256)S(1)}, f32[256]{0:T(256)}, u32[]{:S(2)}) copy-start(f32[256]{0:T(256)} %param.18) | copy-start | bytes 3076
  2.2 28.0 %all-to-all-start = ((bf16[64,4,128]{2,1,0:T(4,128)(2,1)}), bf16[64,4,128]{2,1,0:T(4,128)(2,1)S(1)}, u32[]{:S(2)}, u32[]{:S(2)}) async-start(bf16[64,4,128]{2,1,0:T(4,128)(2,1)} %shard_map.113), calls=%async_computation | async-start | bytes 131072 | tf_op jit(solution)/shard_map/all_to_all | solution.py:201
  18.8 0.7 copy-start.4
  19.5 0.7 copy-start.6
  20.2 0.7 copy-start.8
  20.9 0.7 copy-start.9
  30.2 1.2 %copy-start.1 = (bf16[2048,256]{1,0:T(8,128)(2,1)S(1)}, bf16[2048,256]{1,0:T(8,128)(2,1)}, u32[]{:S(2)}) copy-start(bf16[2048,256]{1,0:T(8,128)(2,1)} %out_weight.1) | copy-start | bytes 3145732
  31.4 1.0 copy-start.2

commit v9 on v7

--- a/solution.py
+++ b/solution.py
@@ -51,13 +51,6 @@
         cost_estimate=pl.CostEstimate(flops=2**26, bytes_accessed=moved, transcendentals=2**18),
         compiler_params=pltpu.CompilerParams(vmem_limit_bytes=limit),
     )
-
-
-def begin(pairs, sems):
-    moves = [pltpu.make_async_copy(a, b, sems.at[i]) for i, (a, b) in enumerate(pairs)]
-    for move in moves:
-        move.start()
-    return moves
 
 
 def copies(queries, out):
@@ -166,30 +159,45 @@
     out[...] = jnp.broadcast_to(dot(features, weight[...]).astype(bf16)[None], out.shape)
 
 
-def normalise(parts, stream_in, gain, out, stream_out, rows):
+def normalise(parts, stream_in, gain, core, out, stream_out, rows):
     for i in range(STEPS):
         rows[ROWS * i : ROWS * (i + 1), :] = stream_in[i]
     stream = rows[...] + jnp.sum(parts[...].astype(f32), axis=0)
     for i in range(STEPS):
         stream_out[i] = stream[ROWS * i : ROWS * (i + 1)]
+    first = core[0] == 0
+    scaled = stream * gain[...]
+    scaled = jnp.where(first, scaled[:, :WIDTH], scaled[:, WIDTH:])
+    stream = jnp.where(first, stream[:, :WIDTH], stream[:, WIDTH:])
     squares = jnp.sum(stream * stream, axis=1, keepdims=True)
     hi, rest = split(squares)
     mid, rest = split(rest)
     at = iota((COUNT, WIDTH), 1) - iota((COUNT, WIDTH), 0)
     stat = jnp.where(at == 0, hi, jnp.where(at == 32, mid, jnp.where(at == 64, rest, 0.0)))
     stat = jnp.broadcast_to(jnp.sum(stat, axis=0, keepdims=True), (8, WIDTH))
-    scaled = stream * gain[...]
-    block = jnp.concatenate([scaled[:, :WIDTH], scaled[:, WIDTH:], stat], axis=0).astype(bf16)
+    block = jnp.concatenate([scaled, stat], axis=0).astype(bf16)
     out[...] = jnp.broadcast_to(block[None], out.shape)
 
 
-def lay(got, tokens, inverse):
-    n = got.shape[0]
-    for s in range(n):
-        for j in range(2):
-            at = (2 * s + j) * WIDTH
-            tokens[:, at : at + WIDTH] = got[s, COUNT * j : COUNT * (j + 1), :]
-    stats = jnp.sum(got[:, 32:40, :].astype(f32), axis=0)
+def lay(own, other, core, tokens, inverse):
+    n = own.shape[0]
+
+    def place(halves):
+        for s in range(n):
+            for j, half in enumerate(halves):
+                at = (2 * s + j) * WIDTH
+                tokens[:, at : at + WIDTH] = half[s, :COUNT, :]
+
+    @pl.when(core[0] == 0)
+    def _():
+        place((own, other))
+
+    @pl.when(core[0] != 0)
+    def _():
+        place((other, own))
+
+    stats = jnp.sum(own[:, COUNT:, :].astype(f32), axis=0)
+    stats = stats + jnp.sum(other[:, COUNT:, :].astype(f32), axis=0)
     stats = jnp.concatenate([stats, stats], axis=0)
     at = iota((COUNT, WIDTH), 1) - iota((COUNT, WIDTH), 0)
     stats = jnp.where((at == 0) | (at == 32) | (at == 64), stats, 0.0)
@@ -222,12 +230,12 @@
     units = gate_up.shape[1]
 
     shape = jax.ShapeDtypeStruct
-    dma = pltpu.SemaphoreType.DMA
     mine = call(copies, shape((seq_count, STEPS, ROWS * QUARTER), bf16), "v")(queries)
     gathered = send(mine, ("z", "y"))
 
     drafted = drafted_key_value.transpose(0, 1, 3, 2, 4).reshape(COUNT, 2, WIDTH)
     index = seq_index.reshape(1)
+    core = lax.axis_index("core").reshape(1)
     bias, fresh_keys, fresh_values = call(
         prepare,
         (
@@ -252,15 +260,17 @@
     )
     scaled, stream = call(
         normalise,
-        (shape((seq_count, 40, WIDTH), bf16), shape((STEPS, ROWS, columns), f32)),
-        "vvv",
+        (shape((seq_count, COUNT + 8, WIDTH), bf16), shape((STEPS, ROWS, columns), f32)),
+        "vvvs",
         [pltpu.VMEM((COUNT, columns), f32)],
-    )(send(partial_sum, ("x", "core")), stream_in, norm_gain.reshape(1, columns))
+    )(send(partial_sum, ("x", "core")), stream_in, norm_gain.reshape(1, columns), core)
+    own = send(scaled, ("z", "y"))
+    other = lax.ppermute(own, "core", [(0, 1), (1, 0)])
     tokens, inverse = call(
         lay,
         (shape((COUNT, seq_count * columns), bf16), shape((COUNT, WIDTH), f32)),
-        "v",
-    )(send(scaled, ("z", "y")))
+        "vvs",
+    )(own, other, core)
     both = jnp.einsum("nc,kfc->knf", tokens, gate_up, preferred_element_type=f32)
     both = both * inverse[None, :, :units]
     hidden = both[0] / (1.0 + jnp.exp(-both[0])) * both[1]

time: 108 us -> 109 us (level)
  the two profiles are of different devices: /device:TPU:8 before, /device:TPU:1 now
where the time goes in v9:
time: 109 us; the launch traced here: 108 us
  blocking collectives  49.5 us (45%)
  starting transfers between devices  30.6 us (28%)
  waiting for transfers between devices  13.9 us (13%)
  local copies, waits for them, and re-layouts  5.81 us (5%)
  Pallas kernels  5.16 us (5%)
  matrix products  2.01 us (2%)
    all_to_all x3, blocking collectives, send(): return lax.all_to_all(x, axis, split_axis=0, concat_axis=0, tiled=True)  49.5 us
    all_to_all x2, starting transfers between devices, send(): return lax.all_to_all(x, axis, split_axis=0, concat_axis=0, tiled=True)  25.5 us
    all_to_all x2, waiting for transfers between devices, send(): return lax.all_to_all(x, axis, split_axis=0, concat_axis=0, tiled=True)  12.6 us
    unnamed x20, local copies, waits for them, and re-layouts  5.8 us
    ppermute x1, starting transfers between devices, shards(): other = lax.ppermute(own, 'core', [(0, 1), (1, 0)])  5.09 us
  transfers between devices with their start and end apart: 3, of which 3 were waited for; matrix products, arithmetic and copies ran while one was open for 0% of the time, Pallas kernels for 1%

profile of v9, /device:TPU:1, one launch (start us, length us, event | category | flops | bytes accessed | tf_op | source)
XLA Modules:
  0.0 108.3 jit_solution(14169941328697381604)
XLA Ops:
  0.6 0.0 copy-start
  0.6 0.0 copy-start.3
  0.7 0.0 copy-start.5
  0.7 0.8 copy-done.5
  1.5 0.7 shard_map.113
  2.2 17.1 %all-to-all-start = ((bf16[64,4,128]{2,1,0:T(4,128)(2,1)}), bf16[64,4,128]{2,1,0:T(4,128)(2,1)S(1)}, u32[]{:S(2)}, u32[]{:S(2)}) async-start(bf16[64,4,128]{2,1,0:T(4,128)(2,1)} %shard_map.113), calls=%async_computation | async-start | bytes 131072 | tf_op jit(solution)/shard_map/all_to_all | solution.py:211
  19.4 0.0 copy-start.4
  19.4 0.7 copy-done.4
  20.1 0.7 copy-done.6
  20.8 0.7 copy-done.8
  21.4 0.7 copy-done.9
  22.1 0.6 shard_map.114
  22.7 7.7 %all-to-all-done.gathered = bf16[64,4,128]{2,1,0:T(4,128)(2,1)S(1)} async-done(((bf16[64,4,128]{2,1,0:T(4,128)(2,1)}), bf16[64,4,128]{2,1,0:T(4,128)(2,1)S(1)}, u32[]{:S(2)}, u32[]{:S(2)}) %all-to-all-start) | async-done | bytes 65568 | tf_op jit(solution)/shard_map/all_to_all | solution.py:211
  30.4 1.0 copy-done.2
  31.5 1.4 %shard_map.115 = bf16[64,8,128]{2,1,0:T(8,128)(2,1)S(1)} custom-call(bf16[64,4,128]{2,1,0:T(4,128)(2,1)S(1)} %all-to-all-done.gathered, bf16[2,1,8,128,128]{4,3,2,1,0:T(8,128)(2,1)S(1)} %copy-done.2, bf16[16,128]{1,0:T(8,128)(2,1)S(1)} %get-tuple-element.9.fresh_keys, bf16[16,128]{1,0:T(8,128)(2,1)S(1)} %get-tuple-element.10.fresh_values, ...), custom_call_target="tpu_custom_call" | custom-call | flops 67108864 | bytes 16777216 | tf_op jit(solution)/shard_map/pallas_call | solution.py:249
  32.9 15.7 %all_to_all.25.got = bf16[64,8,128]{2,1,0:T(8,128)(2,1)S(1)} all-to-all(bf16[64,8,128]{2,1,0:T(8,128)(2,1)S(1)} %shard_map.115), channel_id=1, replica_groups=mesh['x'=4,'core'=2,'z'=8,'y'=8] {'z','y'}, dimensions={0} | all-to-all | bytes 262144 | tf_op jit(solution)/shard_map/all_to_all | solution.py:211
  48.7 0.3 shard_map.116
  49.0 14.9 %all_to_all.26.attended = bf16[64,4,128]{2,1,0:T(4,128)(2,1)S(1)} all-to-all(bf16[64,4,128]{2,1,0:T(4,128)(2,1)S(1)} %shard_map.116), channel_id=1, replica_groups=mesh['x'=4,'core'=2,'z'=8,'y'=8] {'z','y'}, dimensions={0} | all-to-all | bytes 131072 | tf_op jit(solution)/shard_map/all_to_all | solution.py:211
  63.9 1.2 %copy-done.1 = bf16[2048,256]{1,0:T(8,128)(2,1)S(1)} copy-done((bf16[2048,256]{1,0:T(8,128)(2,1)S(1)}, bf16[2048,256]{1,0:T(8,128)(2,1)}, u32[]{:S(2)}) %copy-start.1) | copy-done | bytes 1048600
  65.1 1.2 %shard_map.117 = bf16[8,16,256]{2,1,0:T(8,128)(2,1)} custom-call(bf16[64,4,128]{2,1,0:T(4,128)(2,1)S(1)} %all_to_all.26.attended, bf16[2048,256]{1,0:T(8,128)(2,1)S(1)} %copy-done.1), custom_call_target="tpu_custom_call" | custom-call | flops 67108864 | bytes 16777216 | tf_op jit(solution)/shard_map/pallas_call | solution.py:258
  66.3 8.3 %all-to-all-start.3 = ((bf16[8,16,256]{2,1,0:T(8,128)(2,1)}), bf16[8,16,256]{2,1,0:T(8,128)(2,1)S(1)}, u32[]{:S(2)}, u32[]{:S(2)}) async-start(bf16[8,16,256]{2,1,0:T(8,128)(2,1)} %shard_map.117), calls=%async_computation.3 | async-start | bytes 131072 | tf_op jit(solution)/shard_map/all_to_all | solution.py:211
  74.6 4.9 %all-to-all-done.3.parts = bf16[8,16,256]{2,1,0:T(8,128)(2,1)S(1)} async-done(((bf16[8,16,256]{2,1,0:T(8,128)(2,1)}), bf16[8,16,256]{2,1,0:T(8,128)(2,1)S(1)}, u32[]{:S(2)}, u32[]{:S(2)}) %all-to-all-start.3) | async-done | bytes 65568 | tf_op jit(solution)/shard_map/all_to_all | solution.py:211
  79.5 0.0 copy-done.3
  79.5 0.0 copy-done.7
  79.5 0.6 shard_map.118
  80.1 18.9 %all_to_all.27.own = bf16[64,24,128]{2,1,0:T(8,128)(2,1)S(1)} all-to-all(bf16[64,24,128]{2,1,0:T(8,128)(2,1)S(1)} %get-tuple-element.12), channel_id=1, replica_groups=mesh['x'=4,'core'=2,'z'=8,'y'=8] {'z','y'}, dimensions={0} | all-to-all | bytes 786432 | tf_op jit(solution)/shard_map/all_to_all | solution.py:211
  99.0 5.1 %collective-permute-start = (bf16[64,24,128]{2,1,0:T(8,128)(2,1)S(1)}, bf16[64,24,128]{2,1,0:T(8,128)(2,1)S(1)}, u32[]{:S(2)}, u32[]{:S(2)}) collective-permute-start(bf16[64,24,128]{2,1,0:T(8,128)(2,1)S(1)} %all_to_all.27.own), channel_id=1, source_target_pairs={{0,64},{64,0},{1,65},{65,1},{2,66},{66,2},{3,67},{67,3},{4,68},{68... | collective-permute-start | bytes 1179656 | tf_op jit(solution)/shard_map/ppermute | solution.py:268
  104.1 1.3 %collective-permute-done.other = bf16[64,24,128]{2,1,0:T(8,128)(2,1)S(1)} collective-permute-done((bf16[64,24,128]{2,1,0:T(8,128)(2,1)S(1)}, bf16[64,24,128]{2,1,0:T(8,128)(2,1)S(1)}, u32[]{:S(2)}, u32[]{:S(2)}) %collective-permute-start) | collective-permute-done | bytes 393248 | tf_op jit(solution)/shard_map/ppermute | solution.py:268
  105.4 0.2 shard_map.119
  105.7 0.0 copy-done
  105.7 2.0 %fusion.5 = f32[2,16,52]{2,1,0:T(8,128)S(1)} fusion(bf16[2,52,16384]{2,0,1:T(2,128)(2,1)S(1)} %copy-done, bf16[16,16384]{1,0:T(8,128)(2,1)S(1)} %get-tuple-element.13, f32[16,52]{1,0:T(8,128)S(1)} %bitcast.13), kind=kOutput, calls=%fused_computation.3 | convolution fusion | flops 54527616 | bytes 3942144 | tf_op jit(solution)/shard_map/nc,kfc->knf/dot_general | solution.py:274
  107.7 0.6 multiply_convert_fusion
  (7 shorter events, 0.0 us)
Async XLA Ops:
  0.6 105.0 %copy-start = (bf16[2,52,16384]{2,0,1:T(2,128)(2,1)S(1)}, bf16[2,52,16384]{2,0,1:T(2,128)(2,1)}, u32[]{:S(2)}) copy-start(bf16[2,52,16384]{2,0,1:T(2,128)(2,1)} %param.19) | copy-start | bytes 10223620
  0.6 78.8 %copy-start.3 = (f32[4,4,256]{2,1,0:T(4,128)S(1)}, f32[4,4,256]{2,1,0:T(4,128)}, u32[]{:S(2)}) copy-start(f32[4,4,256]{2,1,0:T(4,128)} %stream_in.1) | copy-start | bytes 49156
  0.7 0.8 copy-start.5
  1.5 78.0 %copy-start.7 = (f32[256]{0:T(256)S(1)}, f32[256]{0:T(256)}, u32[]{:S(2)}) copy-start(f32[256]{0:T(256)} %param.18) | copy-start | bytes 3076
  2.2 28.2 %all-to-all-start = ((bf16[64,4,128]{2,1,0:T(4,128)(2,1)}), bf16[64,4,128]{2,1,0:T(4,128)(2,1)S(1)}, u32[]{:S(2)}, u32[]{:S(2)}) async-start(bf16[64,4,128]{2,1,0:T(4,128)(2,1)} %shard_map.113), calls=%async_computation | async-start | bytes 131072 | tf_op jit(solution)/shard_map/all_to_all | solution.py:211
  19.4 0.7 copy-start.4
  20.1 0.7 copy-start.6
  20.8 0.7 copy-start.8
  21.4 0.7 copy-start.9
  30.4 1.0 copy-start.2
  63.9 1.2 %copy-start.1 = (bf16[2048,256]{1,0:T(8,128)(2,1)S(1)}, bf16[2048,256]{1,0:T(8,128)(2,1)}, u32[]{:S(2)}) copy-start(bf16[2048,256]{1,0:T(8,128)(2,1)} %weight.1) | copy-start | bytes 3145732
  66.3 13.2 %all-to-all-start.3 = ((bf16[8,16,256]{2,1,0:T(8,128)(2,1)}), bf16[8,16,256]{2,1,0:T(8,128)(2,1)S(1)}, u32[]{:S(2)}, u32[]{:S(2)}) async-start(bf16[8,16,256]{2,1,0:T(8,128)(2,1)} %shard_map.117), calls=%async_computation.3 | async-start | bytes 131072 | tf_op jit(solution)/shard_map/all_to_all | solution.py:211
  99.0 6.4 %collective-permute-start = (bf16[64,24,128]{2,1,0:T(8,128)(2,1)S(1)}, bf16[64,24,128]{2,1,0:T(8,128)(2,1)S(1)}, u32[]{:S(2)}, u32[]{:S(2)}) collective-permute-start(bf16[64,24,128]{2,1,0:T(8,128)(2,1)S(1)} %all_to_all.27.own), channel_id=1, source_target_pairs={{0,64},{64,0},{1,65},{65,1},{2,66},{66,2},{3,67},{67,3},{4,68},{68... | collective-permute-start | bytes 1179656 | tf_op jit(solution)/shard_map/ppermute | solution.py:268
